TPU v7x, 256 devices: a whole 4x4x8 slice. The times are simulated.
256 devices in a mesh: conf: 8 (over y_hi, x), orient: 32 (over z, y_lo, core).
Axes of the slice: x: 4, y: 4 (y_hi: 2, y_lo: 2; y = y_hi * 2 + y_lo), z: 8, core: 2. Of those that a mesh axis runs over, the one named last changes fastest.
Arguments:
- particles: bfloat16 [2048, 4096], P(('conf', 'orient')), may hold values from -68 to 68
- defocus_class: int32 [2048], P(('conf', 'orient')), may hold values from 0 to 15
- densities: bfloat16 [64, 4096], P('conf'), may hold values from -6 to 6
- contrast: float32 [16, 4096], replicated, may hold values from -1 to 1
- grid_shift: int32 [3072], P('orient'), may hold values from 0 to 4095
- log_prior: float32 [3072], P('orient'), may hold values from -3 to 0
Outputs:
- loglik: float32 [3, 8, 2048], P(None, None, ('conf', 'orient'))
All inputs are finite; a program needn't handle non-finite values.
Results may differ from a plain program's by a relative error of at most 0.00094.
Values may be sent and summed in bfloat16 or wider, within the bound.
A program may use at most 128 MiB of HBM per device.

v0:
```python
import jax
import jax.numpy as jnp
from jax import lax
from jax.sharding import PartitionSpec as P

SIDE = 64
VISITS = 3


INV_SIXTEEN = 1.0 / 16.0
INV_THIRTY_TWO = 1.0 / 32.0


def passed_along(block, axis, distance):
    devices = range(lax.axis_size(axis))
    route = [((i - distance) % len(devices), i) for i in devices]
    return lax.ppermute(block, axis, route)


def combined_all(value, axis, join):
    pieces = jax.tree.map(lambda part: lax.all_gather(part, axis), value)
    head = jax.tree.map(lambda part: part[0], pieces)
    tail = jax.tree.map(lambda part: part[1:], pieces)
    subtotal, _ = lax.scan(lambda subtotal, slab: (join(subtotal, slab), None), head, tail)
    return subtotal


def projections(local_maps, shift_amount, image_side):
    conf_count = local_maps.shape[0]
    images = local_maps.reshape(conf_count, image_side, image_side)

    def rolled_at(offset):
        return jnp.roll(images, (offset // image_side, offset % image_side), axis=(1, 2))

    panels = jax.vmap(rolled_at, out_axes=1)(shift_amount)
    return panels.reshape(conf_count * shift_amount.shape[0], image_side * image_side)


def excess_power(contrast_sq, panels):
    wide = panels.astype(jnp.float32)
    excess = (wide * wide - 1.0).astype(jnp.bfloat16)
    return lax.dot_general(
        contrast_sq, excess, (((1,), (1,)), ((), ())), preferred_element_type=jnp.float32
    )


def partial_scores(block_rows, block_class, panels, power_table, prior, conf_count):
    class_count = power_table.shape[0]
    correlate = lax.dot_general(
        block_rows, panels, (((1,), (1,)), ((), ())), preferred_element_type=jnp.float32
    )
    onehot = (block_class[:, None] == jnp.arange(class_count, dtype=jnp.int32)[None, :]).astype(
        jnp.float32
    )
    chosen = jnp.dot(onehot, power_table, precision=lax.Precision.HIGHEST)
    score = (correlate * INV_SIXTEEN - chosen * INV_THIRTY_TWO).reshape(
        block_rows.shape[0], conf_count, -1
    ) + prior[None, None, :]
    highest = jnp.max(score, axis=2)
    return (highest, jnp.sum(jnp.exp(score - highest[:, :, None]), axis=2))


def combine(earlier, later):
    highest = jnp.maximum(earlier[0], later[0])
    return (
        highest,
        earlier[1] * jnp.exp(earlier[0] - highest) + later[1] * jnp.exp(later[0] - highest),
    )


def per_device(particles, defocus_class, densities, contrast, grid_shift, log_prior):
    class_count = contrast.shape[0]
    conf_count = densities.shape[0]
    own_count = particles.shape[0]
    contrast_sq = (contrast * contrast).astype(jnp.bfloat16)
    own_onehot = (
        defocus_class[:, None] == jnp.arange(class_count, dtype=jnp.int32)[None, :]
    ).astype(jnp.float32)
    own_envelope = jnp.dot(own_onehot, contrast, precision=lax.Precision.HIGHEST)
    filtered = (particles.astype(jnp.float32) * own_envelope).astype(jnp.bfloat16)
    shard_pair = (filtered, defocus_class)
    partials = []
    panels = projections(densities, grid_shift, SIDE)
    power_table = excess_power(contrast_sq, panels)
    for visit_idx in range(VISITS):
        block_rows, block_class = (
            lax.all_gather(shard_pair[0], "orient", axis=0, tiled=True),
            lax.all_gather(shard_pair[1], "orient", axis=0, tiled=True),
        )
        partials.append(
            partial_scores(block_rows, block_class, panels, power_table, log_prior, conf_count)
        )
        if visit_idx + 1 < VISITS:
            shard_pair = passed_along((shard_pair[0], shard_pair[1]), "conf", 1)
    row_start = lax.axis_index("orient") * own_count
    results = []
    for highest, total in partials:
        merged_top, merged_sum = combined_all((highest, total), "orient", combine)
        results.append(
            lax.dynamic_slice_in_dim(merged_top + jnp.log(merged_sum), row_start, own_count, 0)
        )
    loglik = jnp.stack(results)
    return jnp.transpose(loglik, (0, 2, 1))


def solution(mesh):
    placed = (
        P(("conf", "orient"), None),
        P(("conf", "orient")),
        P("conf", None),
        P(),
        P("orient"),
        P("orient"),
    )
    return jax.shard_map(
        per_device,
        mesh=mesh,
        in_specs=placed,
        out_specs=P(None, None, ("conf", "orient")),
        check_vma=False,
    )
```

profile of v0, /device:TPU:1, one launch (start us, length us, event | category | flops | bytes accessed | tf_op | source)
XLA Modules:
  0.0 431.7 jit_solution(2539111467704048527)
XLA Ops:
  6.5 1.8 fusion.8
  8.4 2.1 collective-permute-start
  10.6 5.8 %collective-permute-done = bf16[8,4096]{1,0:T(8,128)(2,1)S(1)} collective-permute-done((bf16[8,4096]{1,0:T(8,128)(2,1)}, bf16[8,4096]{1,0:T(8,128)(2,1)S(1)}, u32[]{:S(2)}, u32[]{:S(2)}) %collective-permute-start) | collective-permute-done | bytes 65568 | tf_op jit(solution)/shard_map/ppermute | solution.py:17
  17.1 6.9 %collective-permute-done.2 = bf16[8,4096]{1,0:T(8,128)(2,1)S(1)} collective-permute-done((bf16[8,4096]{1,0:T(8,128)(2,1)}, bf16[8,4096]{1,0:T(8,128)(2,1)S(1)}, u32[]{:S(2)}, u32[]{:S(2)}) %collective-permute-start.2) | collective-permute-done | bytes 65568 | tf_op jit(solution)/shard_map/ppermute | solution.py:17
  25.0 1.0 reshape.57
  26.8 7.3 %gather_fusion = bf16[96,8,64,64]{3,1,2,0:T(8,128)(2,1)} fusion(bf16[8,128,64]{2,0,1:T(8,128)(2,1)S(1)} %pad_maximum_fusion.1, s32[96]{0:T(128)S(1)} %fusion.21), kind=kCustom, calls=%fused_computation | custom fusion | bytes 12584064 | tf_op jit(solution)/shard_map/vmap(jit(_roll_dynamic))/gather | solution.py:33
  34.1 16.9 %pad_maximum_fusion = bf16[96,8,64,128]{3,1,2,0:T(8,128)(2,1)} fusion(bf16[96,8,64,64]{3,1,2,0:T(8,128)(2,1)} %gather_fusion), kind=kLoop, calls=%fused_computation.17 | loop fusion | flops 25165824 | bytes 18874368 | tf_op jit(solution)/shard_map/vmap(jit(_roll_dynamic))/concatenate | solution.py:33
  51.0 42.6 %copy.17 = bf16[96,8,64,128]{2,1,0,3:T(8,128)(2,1)} copy(bf16[96,8,64,128]{3,1,2,0:T(8,128)(2,1)} %pad_maximum_fusion) | data formatting | bytes 25165824 | tf_op jit(solution)/shard_map/vmap(jit(_roll_dynamic))/concatenate | solution.py:33
  93.7 18.4 %gather_fusion.1 = bf16[96,8,64,64]{2,1,3,0:T(8,128)(2,1)} fusion(bf16[96,8,64,128]{2,1,0,3:T(8,128)(2,1)} %copy.17, s32[96]{0:T(128)S(1)} %fusion.20), kind=kCustom, calls=%fused_computation.1 | custom fusion | bytes 12584448 | tf_op jit(solution)/shard_map/vmap(jit(_roll_dynamic))/gather | solution.py:33
  112.0 23.2 %copy.18 = bf16[8,96,64,64]{1,0,3,2:T(8,128)(2,1)} copy(bf16[8,96,64,64]{2,0,3,1:T(8,128)(2,1)} %bitcast.78) | data formatting | bytes 12582912 | tf_op jit(solution)/shard_map/vmap()/transpose | solution.py:35
  135.2 13.8 %reshape.58 = bf16[768,4096]{0,1:T(8,128)(2,1)} reshape(bf16[8,96,64,64]{1,0,3,2:T(8,128)(2,1)} %copy.18) | data formatting | bytes 12582912 | tf_op jit(solution)/shard_map/reshape | solution.py:36
  150.5 4.3 %fusion.6 = f32[16,768]{1,0:T(8,128)S(1)} fusion(bf16[768,4096]{0,1:T(8,128)(2,1)} %reshape.58, f32[16,4096]{1,0:T(8,128)S(1)} %copy-done.1), kind=kOutput, calls=%fused_computation.19 | convolution fusion | flops 113377280 | bytes 6602752 | tf_op jit(solution)/shard_map/dot_general | solution.py:42
  155.1 5.8 %collective-permute-done.3 = s32[8]{0:T(128)S(1)} collective-permute-done((s32[8]{0:T(128)S(1)}, s32[8]{0:T(128)S(1)}, u32[]{:S(2)}, u32[]{:S(2)}) %collective-permute-start.3) | collective-permute-done | bytes 64 | tf_op jit(solution)/shard_map/ppermute | solution.py:17
  161.1 20.1 %all-reduce.4 = (s32[256]{0:T(256)S(1)}, s32[256]{0:T(256)S(1)}, s32[256]{0:T(256)S(1)}) all-reduce(s32[256]{0:T(256)S(1)} %dynamic-update-slice, s32[256]{0:T(256)S(1)} %dynamic-update-slice.1, s32[256]{0:T(256)S(1)} %dynamic-update-slice.2), channel_id=1, replica_groups=mesh['conf'=8,'orient'=32] {'orient'}, use_global_device_ids=true, to_apply=%add.1 | all-reduce | flops 768 | bytes 6144
  182.2 5.3 %convolution_multiply_fusion.6 = f32[256,768]{1,0:T(8,128)S(1)} fusion(bf16[256,4096]{1,0:T(8,128)(2,1)} %all-gather.10.cloned.1.call-done, bf16[768,4096]{0,1:T(8,128)(2,1)} %reshape.58), kind=kOutput, calls=%fused_computation.29 | convolution fusion | flops 1610809344 | bytes 9175040 | tf_op jit(solution)/shard_map/dot_general | solution.py:49
  188.4 35.4 %all-gather = f32[8192,8]{0,1:T(8,128)S(1)} all-gather(f32[256,8]{0,1:T(8,128)S(1)} %add_reduce_fusion.2), channel_id=2, replica_groups=mesh['conf'=8,'orient'=32] {'orient'}, dimensions={0}, use_global_device_ids=true | all-gather | bytes 270336 | tf_op jit(solution)/shard_map/all_gather | solution.py:21
  223.8 0.8 slice.72
  224.6 6.1 %fusion.10 = f32[256,768]{1,0:T(8,128)} fusion(f32[256,768]{1,0:T(8,128)S(1)} %convolution_multiply_fusion.2, bf16[256,4096]{1,0:T(8,128)(2,1)} %all-gather.12.cloned.1.call-done, bf16[768,4096]{0,1:T(8,128)(2,1)} %reshape.58), kind=kOutput, calls=%fused_computation.30 | convolution fusion | flops 1611005952 | bytes 9961472 | tf_op jit(solution)/shard_map/dot_general | solution.py:49
  230.7 1.4 copy.21
  232.1 5.2 %fusion.11 = f32[256,768]{1,0:T(8,128)S(1)} fusion(f32[256,768]{1,0:T(8,128)S(1)} %convolution_multiply_fusion.1, bf16[256,4096]{1,0:T(8,128)(2,1)} %all-gather.14.cloned.1.call-done, bf16[768,4096]{0,1:T(8,128)(2,1)} %reshape.58), kind=kOutput, calls=%fused_computation.31 | convolution fusion | flops 1611005952 | bytes 9961472 | tf_op jit(solution)/shard_map/dot_general | solution.py:49
  237.9 32.2 %all-gather.1 = f32[8192,8]{0,1:T(8,128)S(1)} all-gather(f32[256,8]{0,1:T(8,128)S(1)} %get-tuple-element.95), channel_id=3, replica_groups=mesh['conf'=8,'orient'=32] {'orient'}, dimensions={0}, use_global_device_ids=true | all-gather | bytes 270336 | tf_op jit(solution)/shard_map/all_gather | solution.py:21
  270.6 31.9 %all-gather.3 = f32[8192,8]{0,1:T(8,128)S(1)} all-gather(f32[256,8]{0,1:T(8,128)S(1)} %get-tuple-element.98), channel_id=5, replica_groups=mesh['conf'=8,'orient'=32] {'orient'}, dimensions={0}, use_global_device_ids=true | all-gather | bytes 270336 | tf_op jit(solution)/shard_map/all_gather | solution.py:21
  302.5 32.2 %all-gather.2 = f32[8192,8]{0,1:T(8,128)S(1)} all-gather(f32[256,8]{0,1:T(8,128)S(1)} %get-tuple-element.96), channel_id=4, replica_groups=mesh['conf'=8,'orient'=32] {'orient'}, dimensions={0}, use_global_device_ids=true | all-gather | bytes 270336 | tf_op jit(solution)/shard_map/all_gather | solution.py:21
  334.8 31.9 %all-gather.5 = f32[8192,8]{0,1:T(8,128)S(1)} all-gather(f32[256,8]{0,1:T(8,128)S(1)} %get-tuple-element.99), channel_id=7, replica_groups=mesh['conf'=8,'orient'=32] {'orient'}, dimensions={0}, use_global_device_ids=true | all-gather | bytes 270336 | tf_op jit(solution)/shard_map/all_gather | solution.py:21
  366.7 32.2 %all-gather.4 = f32[8192,8]{0,1:T(8,128)S(1)} all-gather(f32[256,8]{0,1:T(8,128)S(1)} %get-tuple-element.97), channel_id=6, replica_groups=mesh['conf'=8,'orient'=32] {'orient'}, dimensions={0}, use_global_device_ids=true | all-gather | bytes 270336 | tf_op jit(solution)/shard_map/all_gather | solution.py:21
  399.0 22.6 %while.36 = (s32[]{:T(128)}, f32[256,8]{0,1:T(8,128)S(1)}, f32[256,8]{0,1:T(8,128)S(1)}, f32[31,256,8]{1,2,0:T(8,128)}, f32[31,256,8]{1,2,0:T(8,128)S(1)}, /*index=5*/s32[]{:T(128)}) while((s32[]{:T(128)}, f32[256,8]{0,1:T(8,128)S(1)}, f32[256,8]{0,1:T(8,128)S(1)}, f32[31,256,8]{1,2,0:T(8,128)}, f32[31,256,8]{1,2,0:T(8,128)S(1)}, ...), condition=%wide.region_3.4_spmd, body=%wide.region_2.3_spmd.sunk | while | flops 12290 | bytes 49225 | solution.py:24
  399.0 0.7 fusion.36
  399.7 0.7 fusion.36
  400.5 0.7 fusion.36
  401.2 0.7 fusion.36
  401.9 0.7 fusion.36
  403.4 0.7 fusion.36
  404.1 0.7 fusion.36
  405.6 0.7 fusion.36
  406.3 0.7 fusion.36
  407.7 0.7 fusion.36
  409.2 0.7 fusion.36
  409.9 0.7 fusion.36
  411.4 0.7 fusion.36
  412.1 0.7 fusion.36
  413.6 0.7 fusion.36
  415.8 0.7 fusion.36
  417.2 0.7 fusion.36
  417.9 0.7 fusion.36
  419.4 0.7 fusion.36
  420.1 0.7 fusion.36
  421.7 1.2 while.37
  422.9 1.3 while.38
  (140 shorter events, 17.0 us)
Async XLA Ops:
  6.5 175.7 %all-gather.10.cloned.1.call-start = ((), (), s32[]{:S(2)}) async-start(), calls=%async_computation | async-start | bytes 2162688 | tf_op jit(solution)/shard_map/all_gather | solution.py:87
  8.4 216.2 %all-gather.12.cloned.1.call-start = ((), (), s32[]{:S(2)}) async-start(), calls=%async_computation.1 | async-start | bytes 2162688 | tf_op jit(solution)/shard_map/all_gather | solution.py:87
  8.4 7.9 %collective-permute-start = (bf16[8,4096]{1,0:T(8,128)(2,1)}, bf16[8,4096]{1,0:T(8,128)(2,1)S(1)}, u32[]{:S(2)}, u32[]{:S(2)}) collective-permute-start(bf16[8,4096]{1,0:T(8,128)(2,1)} %fusion.8), channel_id=1, source_target_pairs={{224,0},{0,32},{32,64},{64,96},{96,128},{128,160},{160,192},{192,2... | collective-permute-start | bytes 196616 | tf_op jit(solution)/shard_map/ppermute | solution.py:17
  16.3 0.6 copy-start.2
  17.0 215.1 %all-gather.14.cloned.1.call-start = ((), (), s32[]{:S(2)}) async-start(), calls=%async_computation.2 | async-start | bytes 2162688 | tf_op jit(solution)/shard_map/all_gather | solution.py:87
  17.0 7.0 %collective-permute-start.2 = (bf16[8,4096]{1,0:T(8,128)(2,1)}, bf16[8,4096]{1,0:T(8,128)(2,1)S(1)}, u32[]{:S(2)}, u32[]{:S(2)}) collective-permute-start(bf16[8,4096]{1,0:T(8,128)(2,1)} %copy-done.2), channel_id=1, source_target_pairs={{224,0},{0,32},{32,64},{64,96},{96,128},{128,160},{160,192},{192,2... | collective-permute-start | bytes 196616 | tf_op jit(solution)/shard_map/ppermute | solution.py:17
  24.1 0.6 copy-start.3
  24.7 130.2 %collective-permute-start.1 = (s32[8]{0:T(128)}, s32[8]{0:T(128)S(1)}, u32[]{:S(2)}, u32[]{:S(2)}) collective-permute-start(s32[8]{0:T(128)} %param.13), channel_id=1, source_target_pairs={{224,0},{0,32},{32,64},{64,96},{96,128},{128,160},{160,192},{192,2... | collective-permute-start | bytes 104 | tf_op jit(solution)/shard_map/ppermute | solution.py:17
  51.0 42.7 %copy-start.6 = (s32[96]{0:T(128)S(1)}, s32[96]{0:T(128)}, u32[]{:S(2)}) copy-start(s32[96]{0:T(128)} %param.16) | copy-start | bytes 1156
  135.2 13.8 %copy-start.7 = (u32[256]{0:T(256)S(1)}, u32[256]{0:T(256)}, u32[]{:S(2)}) copy-start(u32[256]{0:T(256)} %constant.162) | copy-start | bytes 3076
  135.2 15.1 %copy-start.5 = (s32[8]{0:T(128)S(1)}, s32[8]{0:T(128)}, u32[]{:S(2)}) copy-start(s32[8]{0:T(128)} %param.13) | copy-start | bytes 100
  135.2 15.3 %copy-start.1 = (f32[16,4096]{1,0:T(8,128)S(1)}, f32[16,4096]{1,0:T(8,128)}, u32[]{:S(2)}) copy-start(f32[16,4096]{1,0:T(8,128)} %param.15) | copy-start | bytes 786436
  154.9 6.0 %collective-permute-start.3 = (s32[8]{0:T(128)S(1)}, s32[8]{0:T(128)S(1)}, u32[]{:S(2)}, u32[]{:S(2)}) collective-permute-start(s32[8]{0:T(128)S(1)} %collective-permute-done.1), channel_id=1, source_target_pairs={{224,0},{0,32},{32,64},{64,96},{96,128},{128,160},{160,192},{192,2... | collective-permute-start | bytes 104 | tf_op jit(solution)/shard_map/ppermute | solution.py:17
  182.2 6.1 %copy-start.4 = (f32[96]{0:T(128)S(1)}, f32[96]{0:T(128)}, u32[]{:S(2)}) copy-start(f32[96]{0:T(128)} %param.17) | copy-start | bytes 1156
  223.8 13.5 %copy-start = (f32[8192,8]{0,1:T(8,128)}, f32[8192,8]{0,1:T(8,128)S(1)}, u32[]{:S(2)}) copy-start(f32[8192,8]{0,1:T(8,128)S(1)} %all-gather) | copy-start | bytes 786436
  237.6 161.4 %slice-start = ((f32[8192,8]{0,1:T(8,128)}), f32[256,8]{0,1:T(8,128)S(1)}, s32[]{:S(2)}) async-start(f32[8192,8]{0,1:T(8,128)} %copy-done), calls=%async_computation.3 | async-start | bytes 16384 | tf_op jit(solution)/shard_map/slice | solution.py:22
Sparse Core Ops, SparseCore 0:
  9.2 68.8 all-gather.9
  80.0 64.3 all-gather.11
  146.3 64.4 all-gather.13
where the time goes:
time: 434 us; the launch traced here: 432 us
  blocking collectives  216 us (50%)
  local copies, waits for them, and re-layouts  113 us (26%)
  other arithmetic  41.9 us (10%)
  matrix products  24.3 us (6%)
  waiting for transfers between devices  18.5 us (4%)
  between operations  14.1 us (3%)
    all_gather x6, blocking collectives, combined_all(): pieces = jax.tree.map(lambda part: lax.all_gather(part, axis), value)  196 us
    concatenate x1, local copies, waits for them, and re-layouts, rolled_at(): jnp.roll(images, (offset // image_side, offset % image_side), axis=(1, 2))  42.6 us
    gather x2, local copies, waits for them, and re-layouts, rolled_at(): jnp.roll(images, (offset // image_side, offset % image_side), axis=(1, 2))  25.7 us
    add x93, other arithmetic, combine(): earlier[1] * jnp.exp(earlier[0] - highest)  23.3 us
    transpose x1, local copies, waits for them, and re-layouts, projections(): panels = jax.vmap(rolled_at, out_axes=1)(shift_amount)  23.2 us
    unnamed x1, blocking collectives  20.1 us
    ppermute x4, waiting for transfers between devices, passed_along(): return lax.ppermute(block, axis, route)  18.4 us
    concatenate x3, other arithmetic, rolled_at(): jnp.roll(images, (offset // image_side, offset % image_side), axis=(1, 2))  17.6 us
  transfers between devices with their start and end apart: 7, of which 3 were waited for; matrix products, arithmetic and copies ran while one was open for 34% of the time, Pallas kernels for 0%

commit v1 on v0

v1 whole, which is shorter than its diff:
```python
import functools
import math

import jax
import jax.numpy as jnp
import numpy as np
from jax import lax
from jax.experimental import pallas as pl
from jax.experimental.pallas import tpu as pltpu
from jax.sharding import PartitionSpec as P

SIDE = 64
ROWS = 8
LANES = 128
TILES = 32
HALF = TILES // 2 + 1
MESH = pl.DeviceIdType.MESH
F32 = jnp.float32
BF16 = jnp.bfloat16
FAR = -1e30


def lane_matrix():
    yl, x = np.divmod(np.arange(LANES), SIDE)
    phase = 2.0 * np.pi * (np.outer(x, x) % SIDE) / SIDE + np.pi * (np.outer(yl, yl) % 2)
    c, s = np.cos(phase), np.sin(phase)
    full = np.block([[c, s], [-s, c]]).astype(np.float32)
    high = full.astype(jnp.bfloat16)
    low = (full - high.astype(np.float32)).astype(jnp.bfloat16)
    return np.concatenate([high, low], axis=0)


def turned(z, num, den):
    re, im = z
    eighth = (8 * num / den) % 8
    if eighth == 0:
        return z
    if eighth == 2:
        return (-im, re)
    angle = 2.0 * math.pi * num / den
    c, s = math.cos(angle), math.sin(angle)
    if eighth == 1:
        return ((re - im) * c, (re + im) * c)
    if eighth == 3:
        return ((re + im) * c, (im - re) * c)
    return (re * c - im * s, re * s + im * c)


def complex_dft(z):
    n = len(z)
    if n == 1:
        return z
    even, odd = complex_dft(z[0::2]), complex_dft(z[1::2])
    out = [None] * n
    for k in range(n // 2):
        (er, ei), (re, im) = even[k], odd[k]
        if 4 * k == n:
            out[k], out[k + n // 2] = (er - im, ei + re), (er + im, ei - re)
        else:
            tr, ti = turned((re, im), k, n)
            out[k], out[k + n // 2] = (er + tr, ei + ti), (er - tr, ei - ti)
    return out


def real_dft(x):
    n = len(x)
    if n == 2:
        return [(x[0] + x[1], None, False), (x[0] - x[1], None, False)]
    h, q = n // 2, n // 4
    a = [x[j] + x[j + h] for j in range(h)]
    b = [x[j] - x[j + h] for j in range(h)]
    out = [None] * (h + 1)
    out[0::2] = real_dft(a)
    z = complex_dft([turned((b[j], b[j + q]), j, n) for j in range(q)])
    for m in range(q):
        k = 4 * m + 1
        if k <= h:
            out[k] = (*z[m], False)
        else:
            out[n - k] = (*z[m], True)
    return out


def inverse_real_dft(spec):
    h = len(spec) - 1
    n = 2 * h
    if n == 2:
        return [spec[0][0] + spec[1][0], spec[0][0] - spec[1][0]]
    q = n // 4
    even = inverse_real_dft(spec[0::2])
    z = complex_dft([spec[k] if k <= h else spec[n - k] for k in range(1, n, 4)])
    out = [None] * n
    for j in range(q):
        tr, ti = turned(z[j], j, n)
        out[j], out[j + h] = even[j] + tr, even[j] - tr
        out[j + q], out[j + q + h] = even[j + q] - ti, even[j + q] + ti
    return out


def needs_conjugate(k):
    while k % 2 == 0:
        k //= 2
    return k % 4 == 3


def lane_turn(k, scale):
    lane = lax.broadcasted_iota(jnp.int32, (ROWS, LANES), 1)
    angle = 2.0 * math.pi * k / SIDE
    c = jnp.where(lane >= SIDE, F32(scale * math.cos(angle)), F32(scale))
    s = jnp.where(lane >= SIDE, F32(scale * math.sin(angle)), F32(0.0))
    return c, s


def forward_rows(tiles, scale, dst, row):
    spec = real_dft(tiles)
    lane = lax.broadcasted_iota(jnp.int32, (ROWS, LANES), 1)
    rows = pl.ds(row, ROWS)
    zero = jnp.zeros((ROWS, LANES), F32)
    for k, (re, im, conj) in enumerate(spec):
        if k == 0:
            nr, ni = re, zero
        elif k == HALF - 1:
            nr, ni = jnp.where(lane < SIDE, re, 0.0), jnp.where(lane < SIDE, 0.0, re)
        else:
            c, s = lane_turn(k, scale)
            if conj:
                nr, ni = re * c + im * s, re * s - im * c
            else:
                nr, ni = re * c - im * s, re * s + im * c
        dst[k, rows, 0:LANES] = nr
        dst[k, rows, LANES : 2 * LANES] = ni


def split_in_two(x):
    high = x.astype(BF16)
    return high, (x - high.astype(F32)).astype(BF16)


def times_lane_matrix(high, low, w_ref):
    w_high, w_low = w_ref[0 : 2 * LANES, :], w_ref[2 * LANES :, :]
    return jnp.dot(
        jnp.concatenate([high, low, high], axis=1),
        jnp.concatenate([w_high, w_high, w_low], axis=0),
        preferred_element_type=F32,
    )


def forward_lanes(src, w_ref, dst):
    x = src[...].reshape(HALF * 2 * ROWS, 2 * LANES)
    high, low = split_in_two(x)
    dst[...] = times_lane_matrix(high, low, w_ref).reshape(HALF, 2 * ROWS, 2 * LANES)


def log_weights(gath, count):
    shift = gath[:, 0, :].astype(jnp.int32)
    weight = gath[:, 1, :]
    tile, lane = shift // LANES, shift % LANES
    tile_row = lax.broadcasted_iota(jnp.int32, (TILES, LANES), 0)
    lane_row = lax.broadcasted_iota(jnp.int32, (LANES, LANES), 0)
    lefts, rights = [], []
    for r in range(count):
        left = jnp.where(tile_row == tile[r : r + 1, :], weight[r : r + 1, :], 0.0)
        lefts.append(jnp.concatenate(split_in_two(left), axis=0))
        rights.append(jnp.where(lane_row == lane[r : r + 1, :], 1.0, 0.0).astype(BF16))
    both = lax.dot_general(
        jnp.concatenate(lefts, axis=1),
        jnp.concatenate(rights, axis=1),
        (((1,), (1,)), ((), ())),
        preferred_element_type=F32,
    )
    total = both[0:TILES] + both[TILES:]
    return jnp.where(total > 0.0, jnp.log(jnp.where(total > 0.0, total, 1.0)), FAR)


def spectra_product(fr, fi, qr, qi, dr, di, er, ei):
    return (
        fr * dr + fi * di + (qr * er + qi * ei),
        fr * di - fi * dr + (qr * ei - qi * er),
    )


def pair_products(sets, de, lhs, count):
    def one_tile(k, _):
        fq = []
        for ref in sets:
            f, q = ref[k, 0:ROWS, :], ref[k, ROWS : 2 * ROWS, :]
            fq.append((f[:, :LANES], f[:, LANES:], q[:, :LANES], q[:, LANES:]))
        parts = []
        for c in range(count):
            d, e = de[k, c : c + 1, :], de[k, ROWS + c : ROWS + c + 1, :]
            other = (d[:, :LANES], d[:, LANES:], e[:, :LANES], e[:, LANES:])
            for own in fq:
                parts.append(jnp.concatenate(spectra_product(*own, *other), axis=1))
        for i in range(0, len(parts), 2):
            high, low = split_in_two(jnp.concatenate(parts[i : i + 2], axis=0))
            rows = pl.ds(i * ROWS, 2 * ROWS)
            lhs[k, rows, 0 : 2 * LANES] = high
            lhs[k, rows, 2 * LANES :] = low
        return 0

    lax.fori_loop(0, HALF, one_tile, 0)


def inverse_lanes(lhs, w_ref, dst, rows):
    x = lhs[:, 0:rows, :].reshape(HALF * rows, 4 * LANES)
    out = times_lane_matrix(x[:, : 2 * LANES], x[:, 2 * LANES :], w_ref)
    dst[:, 0:rows, :] = out.reshape(HALF, rows, 2 * LANES)


def log_sums(g_ref, lw_ref, ms_ref, groups):
    lane = lax.broadcasted_iota(jnp.int32, (ROWS, LANES), 1)

    def one_group(i, _):
        rows = pl.ds(pl.multiple_of(i * ROWS, ROWS), ROWS)
        spec = []
        for k in range(HALF):
            re, im = g_ref[k, rows, 0:LANES], g_ref[k, rows, LANES : 2 * LANES]
            if k == 0:
                spec.append((re, None))
            elif k == HALF - 1:
                spec.append((jnp.where(lane < SIDE, re, -im), None))
            else:
                c, s = lane_turn(k, 1.0)
                nr = re * c - im * s
                ni = -(re * s) - im * c if needs_conjugate(k) else re * s + im * c
                spec.append((nr, ni))
        score = inverse_real_dft(spec)
        score = [score[j] + lw_ref[j : j + 1, :] for j in range(TILES)]
        top = functools.reduce(jnp.maximum, score)
        total = functools.reduce(jnp.add, [jnp.exp(v - top) for v in score])
        ms_ref[i, 0:ROWS, :] = top
        ms_ref[i, ROWS : 2 * ROWS, :] = total
        return 0

    lax.fori_loop(0, groups, one_group, 0)


def gathered_result(ms_ref, first, step, count):
    lane = lax.broadcasted_iota(jnp.int32, (ROWS, LANES), 1)
    out = jnp.zeros((ROWS, LANES), F32)
    for c in range(count):
        top = ms_ref[first + step * c, 0:ROWS, :]
        total = ms_ref[first + step * c, ROWS : 2 * ROWS, :]
        highest = jnp.max(top, axis=1, keepdims=True)
        summed = jnp.sum(total * jnp.exp(top - highest), axis=1, keepdims=True)
        out = jnp.where(lane == c, highest + jnp.log(summed), out)
    return out.T[0:count, :]


def kernel(
    n_conf,
    n_orient,
    cls_ref,
    part_ref,
    dens_ref,
    con_ref,
    shift_ref,
    prior_ref,
    w_ref,
    out_ref,
    fq_own,
    fq_sib,
    d_send,
    d_recv,
    msg,
    gath,
    stage_a,
    stage_b,
    spec_own,
    spec_sib,
    spec_de,
    lhs,
    g_ref,
    lw_ref,
    ms_ref,
    res_send,
    res_recv,
    gath_send_sem,
    gath_recv_sem,
    big_send_sem,
    big_recv_sem,
    res_send_sem,
    res_recv_sem,
):
    b = lax.axis_index("conf")
    o = lax.axis_index("orient")
    core = lax.rem(o, 2)
    sibling = o + 1 - 2 * core
    reach = 1 + core

    def conf_at(offset):
        return lax.rem(b + offset + 2 * n_conf, n_conf)

    def signal(conf, orient):
        pl.semaphore_signal(
            barrier, inc=1, device_id=(conf, orient), device_id_type=MESH
        )

    barrier = pltpu.get_barrier_semaphore()

    def greet(t, _):
        signal(b, lax.rem(o + t, n_orient))
        return 0

    lax.fori_loop(1, n_orient, greet, 0)
    signal(conf_at(reach), o)
    signal(conf_at(-1), o - core)
    signal(conf_at(-2), o - core + 1)

    row = lax.broadcasted_iota(jnp.int32, (ROWS, LANES), 0)
    cls = jnp.zeros((ROWS, LANES), jnp.int32)
    for i in range(ROWS):
        cls = jnp.where(row == i, cls_ref[i], cls)
    own = [cls == k for k in range(con_ref.shape[0])]
    dens = dens_ref[...].astype(F32)
    d_send[...] = jnp.concatenate(
        [dens[:, : TILES // 2 * LANES], dens[:, TILES // 2 * LANES :]], axis=0
    ).astype(BF16)
    for j in range(TILES):
        cols = slice(j * LANES, (j + 1) * LANES)
        envelope = jnp.zeros((ROWS, LANES), F32)
        for k in range(con_ref.shape[0]):
            envelope = jnp.where(own[k], con_ref[k : k + 1, cols], envelope)
        f = part_ref[:, cols].astype(F32) * envelope
        fq_own[:, cols] = jnp.concatenate([f, envelope * envelope], axis=0).astype(BF16)

    count = shift_ref.shape[0]
    msg[...] = jnp.zeros_like(msg)
    msg[0:1, 0:count] = shift_ref[...].astype(F32).reshape(1, count)
    msg[1:2, 0:count] = jnp.exp(prior_ref[...]).reshape(1, count)
    gath[o] = msg[...]

    pl.semaphore_wait(barrier, n_orient + 2)

    def grid_copy(t):
        return pltpu.make_async_remote_copy(
            src_ref=msg,
            dst_ref=gath.at[o],
            send_sem=gath_send_sem,
            recv_sem=gath_recv_sem,
            device_id=(b, lax.rem(o + t, n_orient)),
            device_id_type=MESH,
        )

    d_copy = pltpu.make_async_remote_copy(
        src_ref=d_send,
        dst_ref=d_recv,
        send_sem=big_send_sem.at[0],
        recv_sem=big_recv_sem.at[0],
        device_id=(conf_at(-reach), o),
        device_id_type=MESH,
    )
    fq_copy = pltpu.make_async_remote_copy(
        src_ref=fq_own,
        dst_ref=fq_sib,
        send_sem=big_send_sem.at[1],
        recv_sem=big_recv_sem.at[1],
        device_id=(b, sibling),
        device_id_type=MESH,
    )
    d_copy.start()
    fq_copy.start()

    def send_grid(t, _):
        grid_copy(t).start()
        return 0

    lax.fori_loop(1, n_orient, send_grid, 0)

    def forward_fq(src, dst):
        for half, scale in ((0, 2.0**-16), (1, -(2.0**-17))):
            tiles = []
            for j in range(TILES):
                both = src[:, j * LANES : (j + 1) * LANES].astype(F32)
                tiles.append(both[half * ROWS : (half + 1) * ROWS] * scale)
            forward_rows(tiles, 2.0, stage_a, half * ROWS)
        forward_lanes(stage_a, w_ref, dst)

    def forward_de(src, dst):
        tiles = []
        for j in range(TILES // 2):
            both = src[:, j * LANES : (j + 1) * LANES].astype(F32)
            tiles.append((both[:ROWS], both[ROWS:]))
        tiles = [t[0] for t in tiles] + [t[1] for t in tiles]
        forward_rows(tiles, 1.0, stage_b, 0)
        excess = [(t * t - 1.0).astype(BF16).astype(F32) for t in tiles]
        forward_rows(excess, 1.0, stage_b, ROWS)
        forward_lanes(stage_b, w_ref, dst)

    forward_fq(fq_own, spec_own)
    forward_de(d_send, spec_de)
    pair_products([spec_own], spec_de, lhs, ROWS)
    inverse_lanes(lhs, w_ref, g_ref, ROWS * ROWS)

    others = pl.ds(0, n_orient - 1)
    everyone = pltpu.make_async_remote_copy(
        src_ref=gath.at[others],
        dst_ref=gath.at[others],
        send_sem=gath_send_sem,
        recv_sem=gath_recv_sem,
        device_id=(b, sibling),
        device_id_type=MESH,
    )
    everyone.wait_recv()
    lw_ref[...] = log_weights(gath, n_orient)
    log_sums(g_ref, lw_ref, ms_ref, ROWS)
    out_ref[0] = gathered_result(ms_ref, 0, 1, ROWS)

    fq_copy.wait_recv()
    forward_fq(fq_sib, spec_sib)
    d_copy.wait_recv()
    forward_de(d_recv, spec_de)
    pair_products([spec_own, spec_sib], spec_de, lhs, ROWS)
    inverse_lanes(lhs, w_ref, g_ref, 2 * ROWS * ROWS)
    log_sums(g_ref, lw_ref, ms_ref, 2 * ROWS)

    res_copies = []
    for p, target in enumerate((o, sibling)):
        res_send[p, :, 0:ROWS] = gathered_result(ms_ref, p, 2, ROWS)
        copy = pltpu.make_async_remote_copy(
            src_ref=res_send.at[p],
            dst_ref=res_recv.at[core],
            send_sem=res_send_sem.at[p],
            recv_sem=res_recv_sem.at[core],
            device_id=(conf_at(reach), target),
            device_id_type=MESH,
        )
        copy.start()
        res_copies.append(copy)

    for v in range(2):
        pltpu.make_async_remote_copy(
            src_ref=res_send.at[v],
            dst_ref=res_recv.at[v],
            send_sem=res_send_sem.at[v],
            recv_sem=res_recv_sem.at[v],
            device_id=(b, sibling),
            device_id_type=MESH,
        ).wait_recv()
        out_ref[1 + v] = res_recv[v, :, 0:ROWS]

    everyone.wait_send()
    d_copy.wait_send()
    fq_copy.wait_send()
    for copy in res_copies:
        copy.wait_send()


def solution(mesh):
    n_conf, n_orient = mesh.shape["conf"], mesh.shape["orient"]
    w = lane_matrix()

    def per_device(particles, defocus_class, densities, contrast, grid_shift, log_prior):
        pix = particles.shape[1]
        vmem = pl.BlockSpec(memory_space=pltpu.VMEM)
        return pl.pallas_call(
            functools.partial(kernel, n_conf, n_orient),
            out_shape=jax.ShapeDtypeStruct((3, ROWS, ROWS), F32),
            in_specs=[pl.BlockSpec(memory_space=pltpu.SMEM)] + [vmem] * 6,
            out_specs=vmem,
            scratch_shapes=[
                pltpu.VMEM((2 * ROWS, pix), BF16),
                pltpu.VMEM((2 * ROWS, pix), BF16),
                pltpu.VMEM((2 * ROWS, pix // 2), BF16),
                pltpu.VMEM((2 * ROWS, pix // 2), BF16),
                pltpu.VMEM((2, LANES), F32),
                pltpu.VMEM((n_orient, 2, LANES), F32),
                pltpu.VMEM((HALF, 2 * ROWS, 2 * LANES), F32),
                pltpu.VMEM((HALF, 2 * ROWS, 2 * LANES), F32),
                pltpu.VMEM((HALF, 2 * ROWS, 2 * LANES), F32),
                pltpu.VMEM((HALF, 2 * ROWS, 2 * LANES), F32),
                pltpu.VMEM((HALF, 2 * ROWS, 2 * LANES), F32),
                pltpu.VMEM((HALF, 2 * ROWS * ROWS, 4 * LANES), BF16),
                pltpu.VMEM((HALF, 2 * ROWS * ROWS, 2 * LANES), F32),
                pltpu.VMEM((TILES, LANES), F32),
                pltpu.VMEM((2 * ROWS, 2 * ROWS, LANES), F32),
                pltpu.VMEM((2, ROWS, LANES), F32),
                pltpu.VMEM((2, ROWS, LANES), F32),
                pltpu.SemaphoreType.DMA,
                pltpu.SemaphoreType.DMA,
                pltpu.SemaphoreType.DMA((2,)),
                pltpu.SemaphoreType.DMA((2,)),
                pltpu.SemaphoreType.DMA((2,)),
                pltpu.SemaphoreType.DMA((2,)),
            ],
            compiler_params=pltpu.CompilerParams(
                collective_id=0, has_side_effects=True, vmem_limit_bytes=48 * 2**20
            ),
        )(defocus_class, particles, densities, contrast, grid_shift, log_prior, jnp.asarray(w))

    placed = (
        P(("conf", "orient"), None),
        P(("conf", "orient")),
        P("conf", None),
        P(),
        P("orient"),
        P("orient"),
    )
    return jax.shard_map(
        per_device,
        mesh=mesh,
        in_specs=placed,
        out_specs=P(None, None, ("conf", "orient")),
        check_vma=False,
    )
```

time: 434 us -> 34.1 us (0.08)
  blocking collectives: 216 us -> 0 us
  local copies, waits for them, and re-layouts: 113 us -> 6.14 us
  other arithmetic: 41.9 us -> 0 us
  Pallas kernels: 0 us -> 27.7 us
  matrix products: 24.3 us -> 0 us
  waiting for transfers between devices: 18.5 us -> 0 us
  between operations: 14.1 us -> 0.02 us
    all_gather x6 -> x0, blocking collectives: 196 us -> none  [combined_all(): pieces = jax.tree.map(lambda part: lax.all_gather(part, axis), value)]
    concatenate x1 -> x0, local copies, waits for them, and re-layouts: 42.6 us -> none  [rolled_at(): jnp.roll(images, (offset // image_side, offset % image_side), axis=(1, 2))]
    pallas_call x0 -> x1, Pallas kernels: none -> 27.7 us  [per_device(): pl.pallas_call(functools.partial(kernel, n_conf, n_orient), out_shape=jax...]
    gather x2 -> x0, local copies, waits for them, and re-layouts: 25.7 us -> none  [rolled_at(): jnp.roll(images, (offset // image_side, offset % image_side), axis=(1, 2))]
    dot_general x8 -> x0, matrix products: 24.3 us -> none  [the longest x3 16.6 us: partial_scores(): lax.dot_general(block_rows, panels, (((1,), (1,)), ((), ())), preferred_e...]
    transpose x2 -> x0, local copies, waits for them, and re-layouts: 23.8 us -> none  [the longest x1 23.2 us: projections(): panels = jax.vmap(rolled_at, out_axes=1)(shift_amount)]
    add x95 -> x0, other arithmetic: 23.4 us -> none  [the longest x93 23.3 us: combine(): earlier[1] * jnp.exp(earlier[0] - highest)]
    unnamed x1 -> x0, blocking collectives: 20.1 us -> none
  transfers between devices with their start and end apart: 7 -> 0, of which waited for: 3 -> 0; matrix products, arithmetic and copies ran while one was open for 34% -> 0% of each run, Pallas kernels for 0% -> 0%
where the time goes in v1:
time: 34.1 us; the launch traced here: 33.9 us
  Pallas kernels  27.7 us (81%)
  local copies, waits for them, and re-layouts  6.14 us (18%)
    pallas_call x1, Pallas kernels, per_device(): pl.pallas_call(functools.partial(kernel, n_conf, n_orient), out_shape=jax...  27.7 us
    unnamed x15, local copies, waits for them, and re-layouts  6.14 us

profile of v1, /device:TPU:1, one launch (start us, length us, event | category | flops | bytes accessed | tf_op | source)
XLA Modules:
  0.0 33.9 jit_solution(3611542093896253193)
XLA Ops:
  0.0 0.0 copy-start
  0.0 0.9 %copy-done = f32[16,4096]{1,0:T(8,128)S(1)} copy-done((f32[16,4096]{1,0:T(8,128)S(1)}, f32[16,4096]{1,0:T(8,128)}, u32[]{:S(2)}) %copy-start) | copy-done | bytes 262168
  1.0 0.0 copy-start.1
  1.0 0.9 %copy-done.1 = bf16[512,256]{1,0:T(8,128)(2,1)S(1)} copy-done((bf16[512,256]{1,0:T(8,128)(2,1)S(1)}, bf16[512,256]{1,0:T(8,128)(2,1)}, u32[]{:S(2)}) %copy-start.1) | copy-done | bytes 262168
  1.9 0.0 copy-start.2
  1.9 0.8 %copy-done.2 = bf16[8,4096]{1,0:T(8,128)(2,1)S(1)} copy-done((bf16[8,4096]{1,0:T(8,128)(2,1)S(1)}, bf16[8,4096]{1,0:T(8,128)(2,1)}, u32[]{:S(2)}) %copy-start.2) | copy-done | bytes 65560
  2.7 0.0 copy-start.3
  2.7 0.8 %copy-done.3 = bf16[8,4096]{1,0:T(8,128)(2,1)S(1)} copy-done((bf16[8,4096]{1,0:T(8,128)(2,1)S(1)}, bf16[8,4096]{1,0:T(8,128)(2,1)}, u32[]{:S(2)}) %copy-start.3) | copy-done | bytes 65560
  3.6 0.0 copy-start.4
  3.6 0.7 %copy-done.4 = s32[8]{0:T(128)S(1)} copy-done((s32[8]{0:T(128)S(1)}, s32[8]{0:T(128)}, u32[]{:S(2)}) %copy-start.4) | copy-done | bytes 56
  4.2 0.0 copy-start.5
  4.2 0.7 %copy-done.5 = s32[96]{0:T(128)S(1)} copy-done((s32[96]{0:T(128)S(1)}, s32[96]{0:T(128)}, u32[]{:S(2)}) %copy-start.5) | copy-done | bytes 408
  4.9 0.0 copy-start.6
  4.9 0.7 %copy-done.6 = f32[96]{0:T(128)S(1)} copy-done((f32[96]{0:T(128)S(1)}, f32[96]{0:T(128)}, u32[]{:S(2)}) %copy-start.6) | copy-done | bytes 408
  5.5 27.7 %shard_map.73 = f32[3,8,8]{2,1,0:T(8,128)S(1)} custom-call(s32[8]{0:T(128)S(1)} %copy-done.4, bf16[8,4096]{1,0:T(8,128)(2,1)S(1)} %copy-done.2, bf16[8,4096]{1,0:T(8,128)(2,1)S(1)} %copy-done.3, f32[16,4096]{1,0:T(8,128)S(1)} %copy-done, s32[96]{0:T(128)S(1)} %copy-done.5, f32[96]{0:T(128)S(1)} %copy-done.6, bf16[512,256]{1,0:T(8,128)(2,1)S(1)} %copy-done.1), custom_call_target="tpu_custom_call" | custom-call | tf_op jit(solution)/shard_map/pallas_call | solution.py:456
  33.3 0.6 %copy.9 = f32[3,8,8]{2,1,0:T(8,128)} copy(f32[3,8,8]{2,1,0:T(8,128)S(1)} %shard_map.73) | data formatting | bytes 1536
Async XLA Ops:
  0.0 0.9 %copy-start = (f32[16,4096]{1,0:T(8,128)S(1)}, f32[16,4096]{1,0:T(8,128)}, u32[]{:S(2)}) copy-start(f32[16,4096]{1,0:T(8,128)} %con_ref.1) | copy-start | bytes 786436
  1.0 0.9 %copy-start.1 = (bf16[512,256]{1,0:T(8,128)(2,1)S(1)}, bf16[512,256]{1,0:T(8,128)(2,1)}, u32[]{:S(2)}) copy-start(bf16[512,256]{1,0:T(8,128)(2,1)} %constant.2.clone.w_ref) | copy-start | bytes 786436
  1.9 0.8 %copy-start.2 = (bf16[8,4096]{1,0:T(8,128)(2,1)S(1)}, bf16[8,4096]{1,0:T(8,128)(2,1)}, u32[]{:S(2)}) copy-start(bf16[8,4096]{1,0:T(8,128)(2,1)} %part_ref.1) | copy-start | bytes 196612
  2.7 0.8 %copy-start.3 = (bf16[8,4096]{1,0:T(8,128)(2,1)S(1)}, bf16[8,4096]{1,0:T(8,128)(2,1)}, u32[]{:S(2)}) copy-start(bf16[8,4096]{1,0:T(8,128)(2,1)} %dens_ref.1) | copy-start | bytes 196612
  3.6 0.7 %copy-start.4 = (s32[8]{0:T(128)S(1)}, s32[8]{0:T(128)}, u32[]{:S(2)}) copy-start(s32[8]{0:T(128)} %cls_ref.1) | copy-start | bytes 100
  4.2 0.7 %copy-start.5 = (s32[96]{0:T(128)S(1)}, s32[96]{0:T(128)}, u32[]{:S(2)}) copy-start(s32[96]{0:T(128)} %shift_ref.1) | copy-start | bytes 1156
  4.9 0.7 %copy-start.6 = (f32[96]{0:T(128)S(1)}, f32[96]{0:T(128)}, u32[]{:S(2)}) copy-start(f32[96]{0:T(128)} %prior_ref.1) | copy-start | bytes 1156

commit v2 on v1

v2 whole, which is shorter than its diff:
```python
import functools
import math

import jax
import jax.numpy as jnp
import numpy as np
from jax import lax
from jax.experimental import pallas as pl
from jax.experimental.pallas import tpu as pltpu
from jax.sharding import PartitionSpec as P

SIDE = 64
ROWS = 8
LANES = 128
TILES = 32
HALF = TILES // 2 + 1
MESH = pl.DeviceIdType.MESH
F32 = jnp.float32
BF16 = jnp.bfloat16
FAR = -1e30
LAYER = 4


def lane_matrix():
    yl, x = np.divmod(np.arange(LANES), SIDE)
    phase = 2.0 * np.pi * (np.outer(x, x) % SIDE) / SIDE + np.pi * (np.outer(yl, yl) % 2)
    c, s = np.cos(phase), np.sin(phase)
    full = np.block([[c, s], [-s, c]]).astype(np.float32)
    high = full.astype(jnp.bfloat16)
    low = (full - high.astype(np.float32)).astype(jnp.bfloat16)
    return np.concatenate([high, low], axis=0)


def turned(z, num, den):
    re, im = z
    eighth = (8 * num / den) % 8
    if eighth == 0:
        return z
    if eighth == 2:
        return (-im, re)
    angle = 2.0 * math.pi * num / den
    c, s = math.cos(angle), math.sin(angle)
    if eighth == 1:
        return ((re - im) * c, (re + im) * c)
    if eighth == 3:
        return ((re + im) * c, (im - re) * c)
    return (re * c - im * s, re * s + im * c)


def complex_dft(z):
    n = len(z)
    if n == 1:
        return z
    even, odd = complex_dft(z[0::2]), complex_dft(z[1::2])
    out = [None] * n
    for k in range(n // 2):
        (er, ei), (re, im) = even[k], odd[k]
        if 4 * k == n:
            out[k], out[k + n // 2] = (er - im, ei + re), (er + im, ei - re)
        else:
            tr, ti = turned((re, im), k, n)
            out[k], out[k + n // 2] = (er + tr, ei + ti), (er - tr, ei - ti)
    return out


def real_dft(x):
    n = len(x)
    if n == 2:
        return [(x[0] + x[1], None, False), (x[0] - x[1], None, False)]
    h, q = n // 2, n // 4
    a = [x[j] + x[j + h] for j in range(h)]
    b = [x[j] - x[j + h] for j in range(h)]
    out = [None] * (h + 1)
    out[0::2] = real_dft(a)
    z = complex_dft([turned((b[j], b[j + q]), j, n) for j in range(q)])
    for m in range(q):
        k = 4 * m + 1
        if k <= h:
            out[k] = (*z[m], False)
        else:
            out[n - k] = (*z[m], True)
    return out


def inverse_real_dft(spec):
    h = len(spec) - 1
    n = 2 * h
    if n == 2:
        return [spec[0][0] + spec[1][0], spec[0][0] - spec[1][0]]
    q = n // 4
    even = inverse_real_dft(spec[0::2])
    z = complex_dft([spec[k] if k <= h else spec[n - k] for k in range(1, n, 4)])
    out = [None] * n
    for j in range(q):
        tr, ti = turned(z[j], j, n)
        out[j], out[j + h] = even[j] + tr, even[j] - tr
        out[j + q], out[j + q + h] = even[j + q] - ti, even[j + q] + ti
    return out


def needs_conjugate(k):
    while k % 2 == 0:
        k //= 2
    return k % 4 == 3


def lane_turn(k, scale):
    lane = lax.broadcasted_iota(jnp.int32, (ROWS, LANES), 1)
    angle = 2.0 * math.pi * k / SIDE
    c = jnp.where(lane >= SIDE, F32(scale * math.cos(angle)), F32(scale))
    s = jnp.where(lane >= SIDE, F32(scale * math.sin(angle)), F32(0.0))
    return c, s


def forward_rows(tiles, scale, dst, row):
    spec = real_dft(tiles)
    lane = lax.broadcasted_iota(jnp.int32, (ROWS, LANES), 1)
    rows = pl.ds(row, ROWS)
    zero = jnp.zeros((ROWS, LANES), F32)
    for k, (re, im, conj) in enumerate(spec):
        if k == 0:
            nr, ni = re, zero
        elif k == HALF - 1:
            nr, ni = jnp.where(lane < SIDE, re, 0.0), jnp.where(lane < SIDE, 0.0, re)
        else:
            c, s = lane_turn(k, scale)
            if conj:
                nr, ni = re * c + im * s, re * s - im * c
            else:
                nr, ni = re * c - im * s, re * s + im * c
        dst[k, rows, 0:LANES] = nr
        dst[k, rows, LANES : 2 * LANES] = ni


def split_in_two(x):
    high = x.astype(BF16)
    return high, (x - high.astype(F32)).astype(BF16)


def times_lane_matrix(high, low, w_ref):
    w_high, w_low = w_ref[0 : 2 * LANES, :], w_ref[2 * LANES :, :]
    return jnp.dot(
        jnp.concatenate([high, low, high], axis=1),
        jnp.concatenate([w_high, w_high, w_low], axis=0),
        preferred_element_type=F32,
    )


def forward_lanes(src, w_ref, dst):
    x = src[...].reshape(HALF * 2 * ROWS, 2 * LANES)
    high, low = split_in_two(x)
    dst[...] = times_lane_matrix(high, low, w_ref).reshape(HALF, 2 * ROWS, 2 * LANES)


def log_weights(gath, count):
    shift = gath[:, 0, :].astype(jnp.int32)
    weight = gath[:, 1, :]
    tile, lane = shift // LANES, shift % LANES
    tile_row = lax.broadcasted_iota(jnp.int32, (TILES, LANES), 0)
    lane_row = lax.broadcasted_iota(jnp.int32, (LANES, LANES), 0)
    lefts, rights = [], []
    for r in range(count):
        left = jnp.where(tile_row == tile[r : r + 1, :], weight[r : r + 1, :], 0.0)
        lefts.append(jnp.concatenate(split_in_two(left), axis=0))
        rights.append(jnp.where(lane_row == lane[r : r + 1, :], 1.0, 0.0).astype(BF16))
    both = lax.dot_general(
        jnp.concatenate(lefts, axis=1),
        jnp.concatenate(rights, axis=1),
        (((1,), (1,)), ((), ())),
        preferred_element_type=F32,
    )
    total = both[0:TILES] + both[TILES:]
    return jnp.where(total > 0.0, jnp.log(jnp.where(total > 0.0, total, 1.0)), FAR)


def spectra_product(fr, fi, qr, qi, dr, di, er, ei):
    return (
        fr * dr + fi * di + (qr * er + qi * ei),
        fr * di - fi * dr + (qr * ei - qi * er),
    )


def pair_products(fq, de, lhs):
    def one_tile(k, _):
        f, q = fq[k, 0:ROWS, :], fq[k, ROWS : 2 * ROWS, :]
        own = (f[:, :LANES], f[:, LANES:], q[:, :LANES], q[:, LANES:])
        parts = []
        for c in range(ROWS):
            d, e = de[k, c : c + 1, :], de[k, ROWS + c : ROWS + c + 1, :]
            other = (d[:, :LANES], d[:, LANES:], e[:, :LANES], e[:, LANES:])
            parts.append(jnp.concatenate(spectra_product(*own, *other), axis=1))
        for i in range(0, len(parts), 2):
            high, low = split_in_two(jnp.concatenate(parts[i : i + 2], axis=0))
            rows = pl.ds(i * ROWS, 2 * ROWS)
            lhs[k, rows, 0 : 2 * LANES] = high
            lhs[k, rows, 2 * LANES :] = low
        return 0

    lax.fori_loop(0, HALF, one_tile, 0)


def inverse_lanes(lhs, w_ref, dst):
    rows = lhs.shape[1]
    x = lhs[...].reshape(HALF * rows, 4 * LANES)
    out = times_lane_matrix(x[:, : 2 * LANES], x[:, 2 * LANES :], w_ref)
    dst[...] = out.reshape(HALF, rows, 2 * LANES)


def scores(g_ref, score_ref, first):
    lane = lax.broadcasted_iota(jnp.int32, (ROWS, LANES), 1)

    def one_group(i, _):
        rows = pl.ds(pl.multiple_of(i * ROWS, ROWS), ROWS)
        spec = []
        for k in range(HALF):
            re, im = g_ref[k, rows, 0:LANES], g_ref[k, rows, LANES : 2 * LANES]
            if k == 0:
                spec.append((re, None))
            elif k == HALF - 1:
                spec.append((jnp.where(lane < SIDE, re, -im), None))
            else:
                c, s = lane_turn(k, 1.0)
                nr = re * c - im * s
                ni = -(re * s) - im * c if needs_conjugate(k) else re * s + im * c
                spec.append((nr, ni))
        for j, value in enumerate(inverse_real_dft(spec)):
            score_ref[first + i, j] = value
        return 0

    lax.fori_loop(0, ROWS, one_group, 0)


def log_sums(score_ref, lw_ref, ms_ref, per_step):
    def some_groups(step, _):
        for p in range(per_step):
            i = step * per_step + p
            value = [score_ref[i, j] + lw_ref[j : j + 1, :] for j in range(TILES)]
            top = functools.reduce(jnp.maximum, value)
            total = functools.reduce(jnp.add, [jnp.exp(v - top) for v in value])
            ms_ref[i, 0:ROWS, :] = top
            ms_ref[i, ROWS : 2 * ROWS, :] = total
        return 0

    lax.fori_loop(0, score_ref.shape[0] // per_step, some_groups, 0)


def results(ms_ref):
    lane = lax.broadcasted_iota(jnp.int32, (ROWS, LANES), 1)
    out = jnp.zeros((ROWS, LANES), F32)
    for i in range(ms_ref.shape[0]):
        top, total = ms_ref[i, 0:ROWS, :], ms_ref[i, ROWS : 2 * ROWS, :]
        highest = jnp.max(top, axis=1, keepdims=True)
        summed = jnp.sum(total * jnp.exp(top - highest), axis=1, keepdims=True)
        out = jnp.where(lane == i, highest + jnp.log(summed), out)
    return out.T


def kernel(
    n_conf,
    n_orient,
    cls_hbm,
    part_hbm,
    dens_hbm,
    con_hbm,
    shift_hbm,
    prior_hbm,
    w_hbm,
    out_ref,
    cls_ref,
    part_ref,
    dens_ref,
    con_ref,
    shift_ref,
    prior_ref,
    w_ref,
    blocks,
    msg,
    gath,
    stage,
    spec_fq,
    spec_de,
    lhs,
    g_ref,
    score_ref,
    lw_ref,
    ms_ref,
    in_sem,
    block_send_sem,
    block_recv_sem,
    grid_send_sem,
    grid_recv_sem,
    lw_send_sem,
    lw_recv_sem,
):
    loads = []
    for i, (src, dst) in enumerate(
        (
            (shift_hbm, shift_ref),
            (prior_hbm, prior_ref),
            (cls_hbm, cls_ref),
            (part_hbm, part_ref),
            (con_hbm, con_ref),
            (dens_hbm, dens_ref),
            (w_hbm, w_ref),
        )
    ):
        loads.append(pltpu.make_async_copy(src, dst, in_sem.at[i]))
        loads[-1].start()

    b = lax.axis_index("conf")
    o = lax.axis_index("orient")
    n_layers = n_orient // LAYER
    n_hubs = n_layers // 2
    z = o // LAYER
    place = lax.rem(o, LAYER)
    is_hub = z < n_hubs

    def conf_at(offset):
        return lax.rem(b + offset + n_conf, n_conf)

    barrier = pltpu.get_barrier_semaphore()

    def greet(conf, orient):
        pl.semaphore_signal(
            barrier, inc=1, device_id=(conf, orient), device_id_type=MESH
        )

    greet(conf_at(-1), o)
    greet(conf_at(-2), o)

    @pl.when(is_hub)
    def _():
        def beside(t, _):
            greet(b, z * LAYER + lax.rem(place + t, LAYER))
            return 0

        def above(t, _):
            greet(b, t)
            return 0

        lax.fori_loop(1, LAYER, beside, 0)
        lax.fori_loop((z + 1) * LAYER, n_orient, above, 0)

    count = shift_ref.shape[0]
    loads[0].wait()
    loads[1].wait()
    msg[...] = jnp.zeros_like(msg)
    msg[0:1, 0:count] = shift_ref[...].astype(F32).reshape(1, count)
    msg[1:2, 0:count] = jnp.exp(prior_ref[...]).reshape(1, count)
    gath[o] = msg[...]

    for load in loads[2:5]:
        load.wait()
    row = lax.broadcasted_iota(jnp.int32, (ROWS, LANES), 0)
    cls = jnp.zeros((ROWS, LANES), jnp.int32)
    for i in range(ROWS):
        cls = jnp.where(row == i, cls_ref[i], cls)

    def envelope_of(classes):
        picked = [classes == k for k in range(con_ref.shape[0])]

        def tile(j):
            out = jnp.zeros((ROWS, LANES), F32)
            for k, mask in enumerate(picked):
                out = jnp.where(mask, con_ref[k : k + 1, j * LANES : (j + 1) * LANES], out)
            return out

        return tile

    envelope = envelope_of(cls)
    half = TILES // 2
    for j in range(half):
        pair = [
            part_ref[:, t * LANES : (t + 1) * LANES].astype(F32) * envelope(t)
            for t in (j, j + half)
        ]
        blocks[0, :, j * LANES : (j + 1) * LANES] = jnp.concatenate(pair, axis=0).astype(BF16)
    blocks[0, :, half * LANES :] = jnp.concatenate([cls, cls], axis=0).astype(F32).astype(BF16)

    pl.semaphore_wait(barrier, 2 + LAYER * jnp.minimum(z, n_hubs) + jnp.where(is_hub, LAYER - 1, 0))

    def send_grid(to):
        pltpu.make_async_remote_copy(
            src_ref=msg,
            dst_ref=gath.at[o],
            send_sem=grid_send_sem,
            recv_sem=grid_recv_sem.at[z],
            device_id=(b, to),
            device_id_type=MESH,
        ).start()

    def send_below(t, _):
        send_grid(t)
        return 0

    def send_beside(t, _):
        send_grid(z * LAYER + lax.rem(place + t, LAYER))
        return 0

    lax.fori_loop(0, LAYER * jnp.minimum(z, n_hubs), send_below, 0)
    lax.fori_loop(1, jnp.where(is_hub, LAYER, 1), send_beside, 0)

    block_copies = []
    for v in (1, 2):
        block_copies.append(
            pltpu.make_async_remote_copy(
                src_ref=blocks.at[0],
                dst_ref=blocks.at[v],
                send_sem=block_send_sem.at[v],
                recv_sem=block_recv_sem.at[v],
                device_id=(conf_at(v), o),
                device_id_type=MESH,
            )
        )
        block_copies[-1].start()

    def grid_wait(layer, number):
        slots = gath.at[pl.ds(layer * LAYER, number)]
        return pltpu.make_async_remote_copy(
            src_ref=slots,
            dst_ref=slots,
            send_sem=grid_send_sem,
            recv_sem=grid_recv_sem.at[layer],
            device_id=(conf_at(1), o),
            device_id_type=MESH,
        )

    def answer(layer):
        @pl.when(z < layer)
        def _():
            grid_wait(layer, LAYER).wait_recv()
            for t in range(LAYER):
                send_grid(layer * LAYER + t)

    def forward(real_tiles, scale, other_tiles, dst):
        forward_rows(real_tiles, scale[0], stage, 0)
        forward_rows(other_tiles, scale[1], stage, ROWS)
        forward_lanes(stage, w_ref, dst)

    loads[5].wait()
    loads[6].wait()
    dens = [dens_ref[:, j * LANES : (j + 1) * LANES].astype(F32) for j in range(TILES)]
    excess = [(t * t - 1.0).astype(BF16).astype(F32) for t in dens]
    forward(dens, (1.0, 1.0), excess, spec_de)

    def visit(v, _):
        @pl.when(v > 0)
        def _():
            pltpu.make_async_remote_copy(
                src_ref=blocks.at[0],
                dst_ref=blocks.at[v],
                send_sem=block_send_sem.at[v],
                recv_sem=block_recv_sem.at[v],
                device_id=(conf_at(1), o),
                device_id_type=MESH,
            ).wait_recv()

        classes = blocks[v, :, half * LANES :].astype(F32)[0:ROWS].astype(jnp.int32)
        tile_of = envelope_of(classes)
        pairs = [blocks[v, :, j * LANES : (j + 1) * LANES].astype(F32) for j in range(half)]
        rows = [p[0:ROWS] for p in pairs] + [p[ROWS:] for p in pairs]
        square = []
        for j in range(TILES):
            e = tile_of(j)
            square.append((e * e).astype(BF16).astype(F32) * -(2.0**-17))
        rows = [r * 2.0**-16 for r in rows]
        forward(rows, (2.0, 2.0), square, spec_fq)
        pair_products(spec_fq, spec_de, lhs)
        inverse_lanes(lhs, w_ref, g_ref)
        scores(g_ref, score_ref, v * ROWS)
        return 0

    lax.fori_loop(0, 2, visit, 0)
    for layer in range(1, n_hubs):
        answer(layer)
    lax.fori_loop(2, 3, visit, 0)

    @pl.when(is_hub)
    def _():
        for layer in range(n_layers):

            @pl.when(z == layer)
            def _():
                grid_wait(layer, LAYER - 1).wait_recv()

            @pl.when((z > layer) | ((z != layer) & (layer >= n_hubs)))
            def _():
                grid_wait(layer, LAYER).wait_recv()

        lw_ref[...] = log_weights(gath, n_orient)

    def lw_copy(layer):
        return pltpu.make_async_remote_copy(
            src_ref=lw_ref,
            dst_ref=lw_ref,
            send_sem=lw_send_sem.at[layer],
            recv_sem=lw_recv_sem,
            device_id=(b, layer * LAYER + place),
            device_id_type=MESH,
        )

    def hub_of(layer):
        return n_hubs - 1 if layer < n_hubs + (n_layers - n_hubs) // 2 else 0

    for layer in range(n_hubs, n_layers):

        @pl.when(z == hub_of(layer))
        def _():
            lw_copy(layer).start()

    @pl.when(jnp.logical_not(is_hub))
    def _():
        pltpu.make_async_remote_copy(
            src_ref=lw_ref,
            dst_ref=lw_ref,
            send_sem=lw_send_sem.at[0],
            recv_sem=lw_recv_sem,
            device_id=(b, place),
            device_id_type=MESH,
        ).wait_recv()

    log_sums(score_ref, lw_ref, ms_ref, 2)
    final = results(ms_ref)
    for v in range(3):
        out_ref[v] = final[v * ROWS : (v + 1) * ROWS, :]

    for layer in range(n_hubs, n_layers):

        @pl.when(z == hub_of(layer))
        def _():
            lw_copy(layer).wait_send()

    @pl.when(is_hub)
    def _():
        grid_wait(0, LAYER * n_hubs - 1).wait_send()

    @pl.when(jnp.logical_not(is_hub))
    def _():
        grid_wait(0, LAYER * n_hubs).wait_send()

    for copy in block_copies:
        copy.wait_send()


def solution(mesh):
    n_conf, n_orient = mesh.shape["conf"], mesh.shape["orient"]
    w = lane_matrix()

    def per_device(*given):
        particles, defocus_class, densities, contrast, grid_shift, log_prior = given
        operands = [
            pltpu.with_memory_space_constraint(x, pltpu.HBM)
            for x in (
                defocus_class,
                particles,
                densities,
                contrast,
                grid_shift,
                log_prior,
                jnp.asarray(w),
            )
        ]
        spectrum = pltpu.VMEM((HALF, 2 * ROWS, 2 * LANES), F32)
        return pl.pallas_call(
            functools.partial(kernel, n_conf, n_orient),
            out_shape=pltpu.VMEM((3, ROWS, ROWS), F32),
            in_specs=[pl.BlockSpec(memory_space=pltpu.HBM)] * 7,
            out_specs=pl.BlockSpec(memory_space=pltpu.VMEM),
            scratch_shapes=[
                pltpu.SMEM(defocus_class.shape, jnp.int32),
                pltpu.VMEM(particles.shape, BF16),
                pltpu.VMEM(densities.shape, BF16),
                pltpu.VMEM(contrast.shape, F32),
                pltpu.VMEM(grid_shift.shape, jnp.int32),
                pltpu.VMEM(log_prior.shape, F32),
                pltpu.VMEM(w.shape, BF16),
                pltpu.VMEM((3, 2 * ROWS, (TILES // 2 + 1) * LANES), BF16),
                pltpu.VMEM((2, LANES), F32),
                pltpu.VMEM((n_orient, 2, LANES), F32),
                spectrum,
                spectrum,
                spectrum,
                pltpu.VMEM((HALF, ROWS * ROWS, 4 * LANES), BF16),
                pltpu.VMEM((HALF, ROWS * ROWS, 2 * LANES), F32),
                pltpu.VMEM((3 * ROWS, TILES, ROWS, LANES), F32),
                pltpu.VMEM((TILES, LANES), F32),
                pltpu.VMEM((3 * ROWS, 2 * ROWS, LANES), F32),
                pltpu.SemaphoreType.DMA((7,)),
                pltpu.SemaphoreType.DMA((3,)),
                pltpu.SemaphoreType.DMA((3,)),
                pltpu.SemaphoreType.DMA,
                pltpu.SemaphoreType.DMA((n_orient // LAYER,)),
                pltpu.SemaphoreType.DMA((n_orient // LAYER,)),
                pltpu.SemaphoreType.DMA,
            ],
            compiler_params=pltpu.CompilerParams(
                collective_id=0, has_side_effects=True, vmem_limit_bytes=56 * 2**20
            ),
        )(*operands)

    placed = (
        P(("conf", "orient"), None),
        P(("conf", "orient")),
        P("conf", None),
        P(),
        P("orient"),
        P("orient"),
    )
    return jax.shard_map(
        per_device,
        mesh=mesh,
        in_specs=placed,
        out_specs=P(None, None, ("conf", "orient")),
        check_vma=False,
    )
```

time: 34.1 us -> 20.4 us (0.60)
  the two profiles are of different devices: /device:TPU:1 before, /device:TPU:160 now
where the time goes in v2:
time: 20.4 us; the launch traced here: 20.3 us
  Pallas kernels  19.7 us (97%)
  local copies, waits for them, and re-layouts  0.6 us (3%)
    pallas_call x1, Pallas kernels, per_device(): pl.pallas_call(functools.partial(kernel, n_conf, n_orient), out_shape=plt...  19.7 us
    unnamed x1, local copies, waits for them, and re-layouts  0.6 us

profile of v2, /device:TPU:160, one launch (start us, length us, event | category | flops | bytes accessed | tf_op | source)
XLA Modules:
  0.0 20.3 jit_solution(16968083489563739030)
XLA Ops:
  0.0 19.7 %shard_map.73 = f32[3,8,8]{2,1,0:T(8,128)S(1)} custom-call(s32[8]{0:T(128)} %cls_hbm.1, bf16[8,4096]{1,0:T(8,128)(2,1)} %part_hbm.1, bf16[8,4096]{1,0:T(8,128)(2,1)} %dens_hbm.1, f32[16,4096]{1,0:T(8,128)} %con_hbm.1, s32[96]{0:T(128)} %shift_hbm.1, f32[96]{0:T(128)} %prior_hbm.1, bf16[512,256]{1,0:T(8,128)(2,1)} %constant.2.clone.w_hbm), custom_call_target="tpu_custom_call" | custom-call | tf_op jit(solution)/shard_map/pallas_call | solution.py:564
  19.7 0.6 %copy.9 = f32[3,8,8]{2,1,0:T(8,128)} copy(f32[3,8,8]{2,1,0:T(8,128)S(1)} %shard_map.73) | data formatting | bytes 1536

commit v3 on v2

--- a/solution.py
+++ b/solution.py
@@ -152,24 +152,33 @@
     dst[...] = times_lane_matrix(high, low, w_ref).reshape(HALF, 2 * ROWS, 2 * LANES)
 
 
-def log_weights(gath, count):
-    shift = gath[:, 0, :].astype(jnp.int32)
-    weight = gath[:, 1, :]
-    tile, lane = shift // LANES, shift % LANES
-    tile_row = lax.broadcasted_iota(jnp.int32, (TILES, LANES), 0)
-    lane_row = lax.broadcasted_iota(jnp.int32, (LANES, LANES), 0)
+def grid_weights(gath, first, count):
+    shift = gath[first : first + count, 0, :].astype(jnp.int32)
+    weight = gath[first : first + count, 1, :]
+    high = weight.astype(BF16).astype(F32)
+    low = weight - high
+    dy, dx = shift // SIDE, shift % SIDE
+    place = dy % 2 * TILES + dy // 2
+    row = lax.broadcasted_iota(jnp.int32, (SIDE, LANES), 0)
     lefts, rights = [], []
     for r in range(count):
-        left = jnp.where(tile_row == tile[r : r + 1, :], weight[r : r + 1, :], 0.0)
-        lefts.append(jnp.concatenate(split_in_two(left), axis=0))
-        rights.append(jnp.where(lane_row == lane[r : r + 1, :], 1.0, 0.0).astype(BF16))
+        mine = row == place[r : r + 1, :]
+        parts = [jnp.where(mine, x[r : r + 1, :], 0.0) for x in (high, low)]
+        lefts.append(jnp.concatenate(parts, axis=0).astype(BF16))
+        right = jnp.where(row == dx[r : r + 1, :], 1.0, 0.0).astype(BF16)
+        rights.append(jnp.concatenate([right, right], axis=0))
     both = lax.dot_general(
         jnp.concatenate(lefts, axis=1),
         jnp.concatenate(rights, axis=1),
         (((1,), (1,)), ((), ())),
         preferred_element_type=F32,
     )
-    total = both[0:TILES] + both[TILES:]
+    total = both[0:SIDE] + both[SIDE:]
+    lane = lax.broadcasted_iota(jnp.int32, (TILES, LANES), 1)
+    return jnp.where(lane < SIDE, total[0:TILES], total[TILES:])
+
+
+def log_or_far(total):
     return jnp.where(total > 0.0, jnp.log(jnp.where(total > 0.0, total, 1.0)), FAR)
 
 
@@ -180,23 +189,20 @@
     )
 
 
-def pair_products(fq, de, lhs):
-    def one_tile(k, _):
+def pair_products(fq, de, first, count, lhs):
+    for k in range(HALF):
         f, q = fq[k, 0:ROWS, :], fq[k, ROWS : 2 * ROWS, :]
         own = (f[:, :LANES], f[:, LANES:], q[:, :LANES], q[:, LANES:])
         parts = []
-        for c in range(ROWS):
+        for c in range(first, first + count):
             d, e = de[k, c : c + 1, :], de[k, ROWS + c : ROWS + c + 1, :]
             other = (d[:, :LANES], d[:, LANES:], e[:, :LANES], e[:, LANES:])
             parts.append(jnp.concatenate(spectra_product(*own, *other), axis=1))
-        for i in range(0, len(parts), 2):
+        for i in range(0, count, 2):
             high, low = split_in_two(jnp.concatenate(parts[i : i + 2], axis=0))
             rows = pl.ds(i * ROWS, 2 * ROWS)
             lhs[k, rows, 0 : 2 * LANES] = high
             lhs[k, rows, 2 * LANES :] = low
-        return 0
-
-    lax.fori_loop(0, HALF, one_tile, 0)
 
 
 def inverse_lanes(lhs, w_ref, dst):
@@ -206,11 +212,10 @@
     dst[...] = out.reshape(HALF, rows, 2 * LANES)
 
 
-def scores(g_ref, score_ref, first):
+def scores(g_ref, score_ref, first, count):
     lane = lax.broadcasted_iota(jnp.int32, (ROWS, LANES), 1)
-
-    def one_group(i, _):
-        rows = pl.ds(pl.multiple_of(i * ROWS, ROWS), ROWS)
+    for i in range(count):
+        rows = pl.ds(i * ROWS, ROWS)
         spec = []
         for k in range(HALF):
             re, im = g_ref[k, rows, 0:LANES], g_ref[k, rows, LANES : 2 * LANES]
@@ -225,9 +230,6 @@
                 spec.append((nr, ni))
         for j, value in enumerate(inverse_real_dft(spec)):
             score_ref[first + i, j] = value
-        return 0
-
-    lax.fori_loop(0, ROWS, one_group, 0)
 
 
 def log_sums(score_ref, lw_ref, ms_ref, per_step):
@@ -279,9 +281,12 @@
     stage,
     spec_fq,
     spec_de,
-    lhs,
-    g_ref,
+    lhs_a,
+    lhs_b,
+    g_a,
+    g_b,
     score_ref,
+    early_ref,
     lw_ref,
     ms_ref,
     in_sem,
@@ -291,6 +296,7 @@
     grid_recv_sem,
     lw_send_sem,
     lw_recv_sem,
+    pair_sem,
 ):
     loads = []
     for i, (src, dst) in enumerate(
@@ -310,9 +316,11 @@
     b = lax.axis_index("conf")
     o = lax.axis_index("orient")
     n_layers = n_orient // LAYER
-    n_hubs = n_layers // 2
+    n_hubs = max(n_layers // 4, 1)
     z = o // LAYER
     place = lax.rem(o, LAYER)
+    core = lax.rem(o, 2)
+    first_core = core == 0
     is_hub = z < n_hubs
 
     def conf_at(offset):
@@ -325,21 +333,28 @@
             barrier, inc=1, device_id=(conf, orient), device_id_type=MESH
         )
 
-    greet(conf_at(-1), o)
-    greet(conf_at(-2), o)
+    def tell_sibling():
+        pl.semaphore_signal(
+            pair_sem, inc=1, device_id=(b, o + 1 - 2 * core), device_id_type=MESH
+        )
+
+    @pl.when(core == 1)
+    def _():
+        greet(b, o - 1)
 
     @pl.when(is_hub)
     def _():
-        def beside(t, _):
-            greet(b, z * LAYER + lax.rem(place + t, LAYER))
+        for t in range(2, LAYER, 2):
+            greet(b, z * LAYER + lax.rem(place - core + t, LAYER))
+
+        def above(t, _):
+            greet(b, 2 * t)
             return 0
 
-        def above(t, _):
-            greet(b, t)
-            return 0
-
-        lax.fori_loop(1, LAYER, beside, 0)
-        lax.fori_loop((z + 1) * LAYER, n_orient, above, 0)
+        lax.fori_loop((z + 1) * (LAYER // 2), n_orient // 2, above, 0)
+
+    greet(conf_at(-1), o - core + 1)
+    greet(conf_at(-2), o - core + 1)
 
     count = shift_ref.shape[0]
     loads[0].wait()
@@ -348,6 +363,38 @@
     msg[0:1, 0:count] = shift_ref[...].astype(F32).reshape(1, count)
     msg[1:2, 0:count] = jnp.exp(prior_ref[...]).reshape(1, count)
     gath[o] = msg[...]
+
+    hubs_below = LAYER * jnp.minimum(z, n_hubs)
+
+    @pl.when(first_core)
+    def _():
+        pl.semaphore_wait(barrier, 1 + hubs_below + jnp.where(is_hub, LAYER - 2, 0))
+        tell_sibling()
+
+    @pl.when(core == 1)
+    def _():
+        pl.semaphore_wait(pair_sem, 1)
+
+    def send_grid(to):
+        pltpu.make_async_remote_copy(
+            src_ref=msg,
+            dst_ref=gath.at[o],
+            send_sem=grid_send_sem,
+            recv_sem=grid_recv_sem.at[z],
+            device_id=(b, to),
+            device_id_type=MESH,
+        ).start()
+
+    def send_below(t, _):
+        send_grid(t)
+        return 0
+
+    def send_beside(t, _):
+        send_grid(z * LAYER + lax.rem(place + t, LAYER))
+        return 0
+
+    lax.fori_loop(0, hubs_below, send_below, 0)
+    lax.fori_loop(1, jnp.where(is_hub, LAYER, 1), send_beside, 0)
 
     for load in loads[2:5]:
         load.wait()
@@ -377,28 +424,14 @@
         blocks[0, :, j * LANES : (j + 1) * LANES] = jnp.concatenate(pair, axis=0).astype(BF16)
     blocks[0, :, half * LANES :] = jnp.concatenate([cls, cls], axis=0).astype(F32).astype(BF16)
 
-    pl.semaphore_wait(barrier, 2 + LAYER * jnp.minimum(z, n_hubs) + jnp.where(is_hub, LAYER - 1, 0))
-
-    def send_grid(to):
-        pltpu.make_async_remote_copy(
-            src_ref=msg,
-            dst_ref=gath.at[o],
-            send_sem=grid_send_sem,
-            recv_sem=grid_recv_sem.at[z],
-            device_id=(b, to),
-            device_id_type=MESH,
-        ).start()
-
-    def send_below(t, _):
-        send_grid(t)
-        return 0
-
-    def send_beside(t, _):
-        send_grid(z * LAYER + lax.rem(place + t, LAYER))
-        return 0
-
-    lax.fori_loop(0, LAYER * jnp.minimum(z, n_hubs), send_below, 0)
-    lax.fori_loop(1, jnp.where(is_hub, LAYER, 1), send_beside, 0)
+    @pl.when(core == 1)
+    def _():
+        pl.semaphore_wait(barrier, 4)
+        tell_sibling()
+
+    @pl.when(first_core)
+    def _():
+        pl.semaphore_wait(pair_sem, 1)
 
     block_copies = []
     for v in (1, 2):
@@ -465,29 +498,39 @@
             square.append((e * e).astype(BF16).astype(F32) * -(2.0**-17))
         rows = [r * 2.0**-16 for r in rows]
         forward(rows, (2.0, 2.0), square, spec_fq)
-        pair_products(spec_fq, spec_de, lhs)
-        inverse_lanes(lhs, w_ref, g_ref)
-        scores(g_ref, score_ref, v * ROWS)
+        part = ROWS // 2
+        pair_products(spec_fq, spec_de, 0, part, lhs_a)
+        inverse_lanes(lhs_a, w_ref, g_a)
+        pair_products(spec_fq, spec_de, part, part, lhs_b)
+        inverse_lanes(lhs_b, w_ref, g_b)
+        scores(g_a, score_ref, v * ROWS, part)
+        scores(g_b, score_ref, v * ROWS + part, part)
         return 0
 
-    lax.fori_loop(0, 2, visit, 0)
+    lax.fori_loop(0, 1, visit, 0)
     for layer in range(1, n_hubs):
         answer(layer)
-    lax.fori_loop(2, 3, visit, 0)
+    lax.fori_loop(1, 3, visit, 0)
 
     @pl.when(is_hub)
     def _():
-        for layer in range(n_layers):
-
-            @pl.when(z == layer)
-            def _():
-                grid_wait(layer, LAYER - 1).wait_recv()
-
-            @pl.when((z > layer) | ((z != layer) & (layer >= n_hubs)))
-            def _():
-                grid_wait(layer, LAYER).wait_recv()
-
-        lw_ref[...] = log_weights(gath, n_orient)
+        def hear(layers):
+            for layer in layers:
+
+                @pl.when(z == layer)
+                def _():
+                    grid_wait(layer, LAYER - 1).wait_recv()
+
+                @pl.when((z > layer) | ((z != layer) & (layer >= n_hubs)))
+                def _():
+                    grid_wait(layer, LAYER).wait_recv()
+
+        middle = n_layers // 2
+        hear(range(middle))
+        early_ref[...] = grid_weights(gath, 0, middle * LAYER)
+        hear(range(middle, n_layers))
+        late = grid_weights(gath, middle * LAYER, n_orient - middle * LAYER)
+        lw_ref[...] = log_or_far(early_ref[...] + late)
 
     def lw_copy(layer):
         return pltpu.make_async_remote_copy(
@@ -500,7 +543,7 @@
         )
 
     def hub_of(layer):
-        return n_hubs - 1 if layer < n_hubs + (n_layers - n_hubs) // 2 else 0
+        return n_hubs - 1 if layer <= n_layers // 2 else 0
 
     for layer in range(n_hubs, n_layers):
 
@@ -519,7 +562,7 @@
             device_id_type=MESH,
         ).wait_recv()
 
-    log_sums(score_ref, lw_ref, ms_ref, 2)
+    log_sums(score_ref, lw_ref, ms_ref, 4)
     final = results(ms_ref)
     for v in range(3):
         out_ref[v] = final[v * ROWS : (v + 1) * ROWS, :]
@@ -580,9 +623,12 @@
                 spectrum,
                 spectrum,
                 spectrum,
-                pltpu.VMEM((HALF, ROWS * ROWS, 4 * LANES), BF16),
-                pltpu.VMEM((HALF, ROWS * ROWS, 2 * LANES), F32),
+                pltpu.VMEM((HALF, ROWS * ROWS // 2, 4 * LANES), BF16),
+                pltpu.VMEM((HALF, ROWS * ROWS // 2, 4 * LANES), BF16),
+                pltpu.VMEM((HALF, ROWS * ROWS // 2, 2 * LANES), F32),
+                pltpu.VMEM((HALF, ROWS * ROWS // 2, 2 * LANES), F32),
                 pltpu.VMEM((3 * ROWS, TILES, ROWS, LANES), F32),
+                pltpu.VMEM((TILES, LANES), F32),
                 pltpu.VMEM((TILES, LANES), F32),
                 pltpu.VMEM((3 * ROWS, 2 * ROWS, LANES), F32),
                 pltpu.SemaphoreType.DMA((7,)),
@@ -592,6 +638,7 @@
                 pltpu.SemaphoreType.DMA((n_orient // LAYER,)),
                 pltpu.SemaphoreType.DMA((n_orient // LAYER,)),
                 pltpu.SemaphoreType.DMA,
+                pltpu.SemaphoreType.REGULAR,
             ],
             compiler_params=pltpu.CompilerParams(
                 collective_id=0, has_side_effects=True, vmem_limit_bytes=56 * 2**20

time: 20.4 us -> 18.8 us (0.922)
  the two profiles are of different devices: /device:TPU:160 before, /device:TPU:72 now
where the time goes in v3:
time: 18.8 us; the launch traced here: 18.7 us
  Pallas kernels  18.1 us (96%)
  local copies, waits for them, and re-layouts  0.6 us (3%)
    pallas_call x1, Pallas kernels, per_device(): pl.pallas_call(functools.partial(kernel, n_conf, n_orient), out_shape=plt...  18.1 us
    unnamed x1, local copies, waits for them, and re-layouts  0.6 us

profile of v3, /device:TPU:72, one launch (start us, length us, event | category | flops | bytes accessed | tf_op | source)
XLA Modules:
  0.0 18.7 jit_solution(14290770385269106025)
XLA Ops:
  0.0 18.1 %shard_map.73 = f32[3,8,8]{2,1,0:T(8,128)S(1)} custom-call(s32[8]{0:T(128)} %cls_hbm.1, bf16[8,4096]{1,0:T(8,128)(2,1)} %part_hbm.1, bf16[8,4096]{1,0:T(8,128)(2,1)} %dens_hbm.1, f32[16,4096]{1,0:T(8,128)} %con_hbm.1, s32[96]{0:T(128)} %shift_hbm.1, f32[96]{0:T(128)} %prior_hbm.1, bf16[512,256]{1,0:T(8,128)(2,1)} %constant.2.clone.w_hbm), custom_call_target="tpu_custom_call" | custom-call | tf_op jit(solution)/shard_map/pallas_call | solution.py:607
  18.1 0.6 %copy.9 = f32[3,8,8]{2,1,0:T(8,128)} copy(f32[3,8,8]{2,1,0:T(8,128)S(1)} %shard_map.73) | data formatting | bytes 1536

commit v4 on v3

--- a/solution.py
+++ b/solution.py
@@ -18,6 +18,7 @@
 F32 = jnp.float32
 BF16 = jnp.bfloat16
 FAR = -1e30
+LOG2E = 1.0 / math.log(2.0)
 LAYER = 4
 
 
@@ -146,10 +147,10 @@
     )
 
 
-def forward_lanes(src, w_ref, dst):
+def forward_lanes(src, w_ref):
     x = src[...].reshape(HALF * 2 * ROWS, 2 * LANES)
     high, low = split_in_two(x)
-    dst[...] = times_lane_matrix(high, low, w_ref).reshape(HALF, 2 * ROWS, 2 * LANES)
+    return times_lane_matrix(high, low, w_ref).reshape(HALF, 2 * ROWS, 2 * LANES)
 
 
 def grid_weights(gath, first, count):
@@ -178,26 +179,25 @@
     return jnp.where(lane < SIDE, total[0:TILES], total[TILES:])
 
 
-def log_or_far(total):
-    return jnp.where(total > 0.0, jnp.log(jnp.where(total > 0.0, total, 1.0)), FAR)
-
-
-def spectra_product(fr, fi, qr, qi, dr, di, er, ei):
-    return (
-        fr * dr + fi * di + (qr * er + qi * ei),
-        fr * di - fi * dr + (qr * ei - qi * er),
-    )
+def log2_or_far(total):
+    some = total > 0.0
+    return jnp.where(some, jnp.log(jnp.where(some, total, 1.0)) / math.log(2.0), FAR)
 
 
 def pair_products(fq, de, first, count, lhs):
     for k in range(HALF):
         f, q = fq[k, 0:ROWS, :], fq[k, ROWS : 2 * ROWS, :]
-        own = (f[:, :LANES], f[:, LANES:], q[:, :LANES], q[:, LANES:])
+        fr, fi, qr, qi = f[:, :LANES], f[:, LANES:], q[:, :LANES], q[:, LANES:]
+        fd, qd = fr - fi, qr - qi
         parts = []
         for c in range(first, first + count):
             d, e = de[k, c : c + 1, :], de[k, ROWS + c : ROWS + c + 1, :]
-            other = (d[:, :LANES], d[:, LANES:], e[:, :LANES], e[:, LANES:])
-            parts.append(jnp.concatenate(spectra_product(*own, *other), axis=1))
+            dr, ds, dm = (d[:, i * LANES : (i + 1) * LANES] for i in range(3))
+            er, es, em = (e[:, i * LANES : (i + 1) * LANES] for i in range(3))
+            shared = dr * fd + er * qd
+            re = shared + (fi * ds + qi * es)
+            im = shared + (fr * dm + qr * em)
+            parts.append(jnp.concatenate([re, im], axis=1))
         for i in range(0, count, 2):
             high, low = split_in_two(jnp.concatenate(parts[i : i + 2], axis=0))
             rows = pl.ds(i * ROWS, 2 * ROWS)
@@ -232,13 +232,21 @@
             score_ref[first + i, j] = value
 
 
+def tree(join, values):
+    while len(values) > 1:
+        values = [join(*values[i : i + 2]) for i in range(0, len(values) - 1, 2)] + (
+            [values[-1]] if len(values) % 2 else []
+        )
+    return values[0]
+
+
 def log_sums(score_ref, lw_ref, ms_ref, per_step):
     def some_groups(step, _):
         for p in range(per_step):
             i = step * per_step + p
             value = [score_ref[i, j] + lw_ref[j : j + 1, :] for j in range(TILES)]
-            top = functools.reduce(jnp.maximum, value)
-            total = functools.reduce(jnp.add, [jnp.exp(v - top) for v in value])
+            top = tree(jnp.maximum, value)
+            total = tree(jnp.add, [jnp.exp2(v - top) for v in value])
             ms_ref[i, 0:ROWS, :] = top
             ms_ref[i, ROWS : 2 * ROWS, :] = total
         return 0
@@ -248,13 +256,15 @@
 
 def results(ms_ref):
     lane = lax.broadcasted_iota(jnp.int32, (ROWS, LANES), 1)
-    out = jnp.zeros((ROWS, LANES), F32)
+    tops = jnp.zeros((ROWS, LANES), F32)
+    sums = jnp.ones((ROWS, LANES), F32)
     for i in range(ms_ref.shape[0]):
         top, total = ms_ref[i, 0:ROWS, :], ms_ref[i, ROWS : 2 * ROWS, :]
         highest = jnp.max(top, axis=1, keepdims=True)
-        summed = jnp.sum(total * jnp.exp(top - highest), axis=1, keepdims=True)
-        out = jnp.where(lane == i, highest + jnp.log(summed), out)
-    return out.T
+        summed = jnp.sum(total * jnp.exp2(top - highest), axis=1, keepdims=True)
+        tops = jnp.where(lane == i, highest, tops)
+        sums = jnp.where(lane == i, summed, sums)
+    return (tops * math.log(2.0) + jnp.log(sums)).T
 
 
 def kernel(
@@ -286,6 +296,7 @@
     g_a,
     g_b,
     score_ref,
+    csq_ref,
     early_ref,
     lw_ref,
     ms_ref,
@@ -298,6 +309,40 @@
     lw_recv_sem,
     pair_sem,
 ):
+    b = lax.axis_index("conf")
+    o = lax.axis_index("orient")
+    n_layers = n_orient // LAYER
+    n_hubs = max(n_layers // 4, 1)
+    z = o // LAYER
+    place = lax.rem(o, LAYER)
+    core = lax.rem(o, 2)
+    first_core = core == 0
+    is_hub = z < n_hubs
+
+    def conf_at(offset):
+        return lax.rem(b + offset + n_conf, n_conf)
+
+    barrier = pltpu.get_barrier_semaphore()
+
+    def greet(conf, orient):
+        pl.semaphore_signal(
+            barrier, inc=1, device_id=(conf, orient), device_id_type=MESH
+        )
+
+    def tell_sibling():
+        pl.semaphore_signal(
+            pair_sem, inc=1, device_id=(b, o + 1 - 2 * core), device_id_type=MESH
+        )
+
+    x = lax.rem(b, n_conf // 2)
+    last_x = x == n_conf // 2 - 1
+
+    @pl.when(x != 1)
+    def _():
+        greet(conf_at(-2), o - core + 1)
+
+    greet(conf_at(-1), o - core + 1)
+
     loads = []
     for i, (src, dst) in enumerate(
         (
@@ -313,31 +358,6 @@
         loads.append(pltpu.make_async_copy(src, dst, in_sem.at[i]))
         loads[-1].start()
 
-    b = lax.axis_index("conf")
-    o = lax.axis_index("orient")
-    n_layers = n_orient // LAYER
-    n_hubs = max(n_layers // 4, 1)
-    z = o // LAYER
-    place = lax.rem(o, LAYER)
-    core = lax.rem(o, 2)
-    first_core = core == 0
-    is_hub = z < n_hubs
-
-    def conf_at(offset):
-        return lax.rem(b + offset + n_conf, n_conf)
-
-    barrier = pltpu.get_barrier_semaphore()
-
-    def greet(conf, orient):
-        pl.semaphore_signal(
-            barrier, inc=1, device_id=(conf, orient), device_id_type=MESH
-        )
-
-    def tell_sibling():
-        pl.semaphore_signal(
-            pair_sem, inc=1, device_id=(b, o + 1 - 2 * core), device_id_type=MESH
-        )
-
     @pl.when(core == 1)
     def _():
         greet(b, o - 1)
@@ -352,9 +372,6 @@
             return 0
 
         lax.fori_loop((z + 1) * (LAYER // 2), n_orient // 2, above, 0)
-
-    greet(conf_at(-1), o - core + 1)
-    greet(conf_at(-2), o - core + 1)
 
     count = shift_ref.shape[0]
     loads[0].wait()
@@ -403,18 +420,14 @@
     for i in range(ROWS):
         cls = jnp.where(row == i, cls_ref[i], cls)
 
-    def envelope_of(classes):
-        picked = [classes == k for k in range(con_ref.shape[0])]
-
-        def tile(j):
-            out = jnp.zeros((ROWS, LANES), F32)
-            for k, mask in enumerate(picked):
-                out = jnp.where(mask, con_ref[k : k + 1, j * LANES : (j + 1) * LANES], out)
-            return out
-
-        return tile
-
-    envelope = envelope_of(cls)
+    picked = [cls == k for k in range(con_ref.shape[0])]
+
+    def envelope(j):
+        out = jnp.zeros((ROWS, LANES), F32)
+        for k, mask in enumerate(picked):
+            out = jnp.where(mask, con_ref[k : k + 1, j * LANES : (j + 1) * LANES], out)
+        return out
+
     half = TILES // 2
     for j in range(half):
         pair = [
@@ -424,28 +437,37 @@
         blocks[0, :, j * LANES : (j + 1) * LANES] = jnp.concatenate(pair, axis=0).astype(BF16)
     blocks[0, :, half * LANES :] = jnp.concatenate([cls, cls], axis=0).astype(F32).astype(BF16)
 
-    @pl.when(core == 1)
-    def _():
-        pl.semaphore_wait(barrier, 4)
-        tell_sibling()
-
-    @pl.when(first_core)
-    def _():
-        pl.semaphore_wait(pair_sem, 1)
-
-    block_copies = []
-    for v in (1, 2):
-        block_copies.append(
-            pltpu.make_async_remote_copy(
-                src_ref=blocks.at[0],
-                dst_ref=blocks.at[v],
-                send_sem=block_send_sem.at[v],
-                recv_sem=block_recv_sem.at[v],
-                device_id=(conf_at(v), o),
-                device_id_type=MESH,
-            )
+    def block_copy(src, dst, to):
+        return pltpu.make_async_remote_copy(
+            src_ref=blocks.at[src],
+            dst_ref=blocks.at[dst],
+            send_sem=block_send_sem.at[2 * src + to - 1],
+            recv_sem=block_recv_sem.at[dst],
+            device_id=(conf_at(to), o),
+            device_id_type=MESH,
         )
-        block_copies[-1].start()
+
+    first_copy, second_copy, passed_copy = (
+        block_copy(0, 1, 1),
+        block_copy(0, 2, 2),
+        block_copy(1, 2, 1),
+    )
+
+    def send_blocks():
+        @pl.when(core == 1)
+        def _():
+            pl.semaphore_wait(barrier, jnp.where(last_x, 2, 4))
+            tell_sibling()
+
+        @pl.when(first_core)
+        def _():
+            pl.semaphore_wait(pair_sem, 1)
+
+        first_copy.start()
+        pl.when(jnp.logical_not(last_x))(second_copy.start)
+
+    send_early = b >= n_conf - 2
+    pl.when(send_early)(send_blocks)
 
     def grid_wait(layer, number):
         slots = gath.at[pl.ds(layer * LAYER, number)]
@@ -465,19 +487,99 @@
             for t in range(LAYER):
                 send_grid(layer * LAYER + t)
 
-    def forward(real_tiles, scale, other_tiles, dst):
-        forward_rows(real_tiles, scale[0], stage, 0)
-        forward_rows(other_tiles, scale[1], stage, ROWS)
-        forward_lanes(stage, w_ref, dst)
+    def forward(tiles, other_tiles, scale):
+        forward_rows(tiles, scale, stage, 0)
+        forward_rows(other_tiles, scale, stage, ROWS)
+        return forward_lanes(stage, w_ref)
 
     loads[5].wait()
     loads[6].wait()
     dens = [dens_ref[:, j * LANES : (j + 1) * LANES].astype(F32) for j in range(TILES)]
     excess = [(t * t - 1.0).astype(BF16).astype(F32) for t in dens]
-    forward(dens, (1.0, 1.0), excess, spec_de)
-
-    def visit(v, _):
-        @pl.when(v > 0)
+    de = forward(dens, excess, 1.0)
+    dr, di = de[:, :, :LANES], de[:, :, LANES:]
+    spec_de[...] = jnp.concatenate([dr, dr + di, di - dr], axis=2)
+    con = con_ref[...]
+    csq_ref[...] = (con * con).astype(BF16)
+
+    def visit(v):
+        n_cls = csq_ref.shape[0]
+        classes = blocks[v, :, half * LANES :].astype(F32)[0:ROWS, 0:n_cls]
+        column = lax.broadcasted_iota(jnp.int32, (ROWS, n_cls), 1).astype(F32)
+        picks = jnp.where(classes == column, 1.0, 0.0).astype(BF16)
+        squares = jnp.dot(picks, csq_ref[...], preferred_element_type=F32)
+        pairs = [blocks[v, :, j * LANES : (j + 1) * LANES].astype(F32) for j in range(half)]
+        rows = [p[0:ROWS] for p in pairs] + [p[ROWS:] for p in pairs]
+        rows = [r * (LOG2E * 2.0**-16) for r in rows]
+        others = [
+            squares[:, j * LANES : (j + 1) * LANES] * (-LOG2E * 2.0**-17) for j in range(TILES)
+        ]
+        spec_fq[...] = forward(rows, others, 2.0)
+        part = ROWS // 2
+        pair_products(spec_fq, spec_de, 0, part, lhs_a)
+        inverse_lanes(lhs_a, w_ref, g_a)
+        pair_products(spec_fq, spec_de, part, part, lhs_b)
+        inverse_lanes(lhs_b, w_ref, g_b)
+        scores(g_a, score_ref, v * ROWS, part)
+        scores(g_b, score_ref, v * ROWS + part, part)
+
+    def lw_copy(layer):
+        return pltpu.make_async_remote_copy(
+            src_ref=lw_ref,
+            dst_ref=lw_ref,
+            send_sem=lw_send_sem.at[layer],
+            recv_sem=lw_recv_sem,
+            device_id=(b, layer * LAYER + place),
+            device_id_type=MESH,
+        )
+
+    def hub_of(layer):
+        return n_hubs - 1 if layer <= n_layers // 2 else 0
+
+    def hear(layers):
+        for layer in layers:
+
+            @pl.when(z == layer)
+            def _():
+                grid_wait(layer, LAYER - 1).wait_recv()
+
+            @pl.when((z > layer) | ((z != layer) & (layer >= n_hubs)))
+            def _():
+                grid_wait(layer, LAYER).wait_recv()
+
+    early = max(n_layers // 2 - 1, 1)
+
+    def make_weights():
+        last = (early + n_layers + 1) // 2
+        total = early_ref[...]
+        for first, end in ((last, n_layers), (early, last)):
+            hear(range(first, end))
+            total = total + grid_weights(gath, first * LAYER, (end - first) * LAYER)
+        lw_ref[...] = log2_or_far(total)
+        for layer in range(n_hubs, n_layers):
+
+            @pl.when(z == hub_of(layer))
+            def _():
+                lw_copy(layer).start()
+
+    visit(0)
+    pl.when(jnp.logical_not(send_early))(send_blocks)
+    for layer in range(1, n_hubs):
+        answer(layer)
+
+    @pl.when(is_hub)
+    def _():
+        hear(range(early))
+        early_ref[...] = grid_weights(gath, 0, early * LAYER)
+
+    weights_at = jnp.where((x == 1) | ((x == 0) & (z > 0)), 2, 3)
+
+    def step(v, _):
+        @pl.when(is_hub & (weights_at == v))
+        def _():
+            make_weights()
+
+        @pl.when(v < 3)
         def _():
             pltpu.make_async_remote_copy(
                 src_ref=blocks.at[0],
@@ -487,69 +589,12 @@
                 device_id=(conf_at(1), o),
                 device_id_type=MESH,
             ).wait_recv()
-
-        classes = blocks[v, :, half * LANES :].astype(F32)[0:ROWS].astype(jnp.int32)
-        tile_of = envelope_of(classes)
-        pairs = [blocks[v, :, j * LANES : (j + 1) * LANES].astype(F32) for j in range(half)]
-        rows = [p[0:ROWS] for p in pairs] + [p[ROWS:] for p in pairs]
-        square = []
-        for j in range(TILES):
-            e = tile_of(j)
-            square.append((e * e).astype(BF16).astype(F32) * -(2.0**-17))
-        rows = [r * 2.0**-16 for r in rows]
-        forward(rows, (2.0, 2.0), square, spec_fq)
-        part = ROWS // 2
-        pair_products(spec_fq, spec_de, 0, part, lhs_a)
-        inverse_lanes(lhs_a, w_ref, g_a)
-        pair_products(spec_fq, spec_de, part, part, lhs_b)
-        inverse_lanes(lhs_b, w_ref, g_b)
-        scores(g_a, score_ref, v * ROWS, part)
-        scores(g_b, score_ref, v * ROWS + part, part)
+            pl.when((v == 1) & (x == 0))(passed_copy.start)
+            visit(v)
+
         return 0
 
-    lax.fori_loop(0, 1, visit, 0)
-    for layer in range(1, n_hubs):
-        answer(layer)
-    lax.fori_loop(1, 3, visit, 0)
-
-    @pl.when(is_hub)
-    def _():
-        def hear(layers):
-            for layer in layers:
-
-                @pl.when(z == layer)
-                def _():
-                    grid_wait(layer, LAYER - 1).wait_recv()
-
-                @pl.when((z > layer) | ((z != layer) & (layer >= n_hubs)))
-                def _():
-                    grid_wait(layer, LAYER).wait_recv()
-
-        middle = n_layers // 2
-        hear(range(middle))
-        early_ref[...] = grid_weights(gath, 0, middle * LAYER)
-        hear(range(middle, n_layers))
-        late = grid_weights(gath, middle * LAYER, n_orient - middle * LAYER)
-        lw_ref[...] = log_or_far(early_ref[...] + late)
-
-    def lw_copy(layer):
-        return pltpu.make_async_remote_copy(
-            src_ref=lw_ref,
-            dst_ref=lw_ref,
-            send_sem=lw_send_sem.at[layer],
-            recv_sem=lw_recv_sem,
-            device_id=(b, layer * LAYER + place),
-            device_id_type=MESH,
-        )
-
-    def hub_of(layer):
-        return n_hubs - 1 if layer <= n_layers // 2 else 0
-
-    for layer in range(n_hubs, n_layers):
-
-        @pl.when(z == hub_of(layer))
-        def _():
-            lw_copy(layer).start()
+    lax.fori_loop(1, 4, step, 0)
 
     @pl.when(jnp.logical_not(is_hub))
     def _():
@@ -581,8 +626,9 @@
     def _():
         grid_wait(0, LAYER * n_hubs).wait_send()
 
-    for copy in block_copies:
-        copy.wait_send()
+    first_copy.wait_send()
+    pl.when(jnp.logical_not(last_x))(second_copy.wait_send)
+    pl.when(x == 0)(passed_copy.wait_send)
 
 
 def solution(mesh):
@@ -622,17 +668,18 @@
                 pltpu.VMEM((n_orient, 2, LANES), F32),
                 spectrum,
                 spectrum,
-                spectrum,
+                pltpu.VMEM((HALF, 2 * ROWS, 3 * LANES), F32),
                 pltpu.VMEM((HALF, ROWS * ROWS // 2, 4 * LANES), BF16),
                 pltpu.VMEM((HALF, ROWS * ROWS // 2, 4 * LANES), BF16),
                 pltpu.VMEM((HALF, ROWS * ROWS // 2, 2 * LANES), F32),
                 pltpu.VMEM((HALF, ROWS * ROWS // 2, 2 * LANES), F32),
                 pltpu.VMEM((3 * ROWS, TILES, ROWS, LANES), F32),
+                pltpu.VMEM(contrast.shape, BF16),
                 pltpu.VMEM((TILES, LANES), F32),
                 pltpu.VMEM((TILES, LANES), F32),
                 pltpu.VMEM((3 * ROWS, 2 * ROWS, LANES), F32),
                 pltpu.SemaphoreType.DMA((7,)),
-                pltpu.SemaphoreType.DMA((3,)),
+                pltpu.SemaphoreType.DMA((4,)),
                 pltpu.SemaphoreType.DMA((3,)),
                 pltpu.SemaphoreType.DMA,
                 pltpu.SemaphoreType.DMA((n_orient // LAYER,)),

time: 18.8 us -> 16.6 us (0.88)
  the two profiles are of different devices: /device:TPU:72 before, /device:TPU:1 now
where the time goes in v4:
time: 16.6 us; the launch traced here: 16.4 us
  Pallas kernels  15.8 us (95%)
  local copies, waits for them, and re-layouts  0.6 us (4%)
    pallas_call x1, Pallas kernels, per_device(): pl.pallas_call(functools.partial(kernel, n_conf, n_orient), out_shape=plt...  15.8 us
    unnamed x1, local copies, waits for them, and re-layouts  0.6 us

profile of v4, /device:TPU:1, one launch (start us, length us, event | category | flops | bytes accessed | tf_op | source)
XLA Modules:
  0.0 16.4 jit_solution(10711820548216090775)
XLA Ops:
  0.0 15.8 %shard_map.73 = f32[3,8,8]{2,1,0:T(8,128)S(1)} custom-call(s32[8]{0:T(128)} %cls_hbm.1, bf16[8,4096]{1,0:T(8,128)(2,1)} %part_hbm.1, bf16[8,4096]{1,0:T(8,128)(2,1)} %dens_hbm.1, f32[16,4096]{1,0:T(8,128)} %con_hbm.1, s32[96]{0:T(128)} %shift_hbm.1, f32[96]{0:T(128)} %prior_hbm.1, bf16[512,256]{1,0:T(8,128)(2,1)} %constant.2.clone.w_hbm), custom_call_target="tpu_custom_call" | custom-call | tf_op jit(solution)/shard_map/pallas_call | solution.py:653
  15.8 0.6 %copy.9 = f32[3,8,8]{2,1,0:T(8,128)} copy(f32[3,8,8]{2,1,0:T(8,128)S(1)} %shard_map.73) | data formatting | bytes 1536

commit v5 on v4

--- a/solution.py
+++ b/solution.py
@@ -105,32 +105,49 @@
     return k % 4 == 3
 
 
-def lane_turn(k, scale):
+def by_half(first, second):
     lane = lax.broadcasted_iota(jnp.int32, (ROWS, LANES), 1)
-    angle = 2.0 * math.pi * k / SIDE
-    c = jnp.where(lane >= SIDE, F32(scale * math.cos(angle)), F32(scale))
-    s = jnp.where(lane >= SIDE, F32(scale * math.sin(angle)), F32(0.0))
-    return c, s
-
-
-def forward_rows(tiles, scale, dst, row):
+    return jnp.where(lane >= SIDE, F32(second), F32(first))
+
+
+def forward_rows(tiles, dst, row, scale=1.0, for_products=False):
     spec = real_dft(tiles)
-    lane = lax.broadcasted_iota(jnp.int32, (ROWS, LANES), 1)
     rows = pl.ds(row, ROWS)
     zero = jnp.zeros((ROWS, LANES), F32)
+    lane = lax.broadcasted_iota(jnp.int32, (ROWS, LANES), 1)
     for k, (re, im, conj) in enumerate(spec):
+        if im is None:
+            re = re if scale == 1.0 else re * scale
         if k == 0:
             nr, ni = re, zero
         elif k == HALF - 1:
             nr, ni = jnp.where(lane < SIDE, re, 0.0), jnp.where(lane < SIDE, 0.0, re)
         else:
-            c, s = lane_turn(k, scale)
+            angle = 2.0 * math.pi * k / SIDE
+            if for_products:
+                h = math.cos(angle / 2.0) * 2.0 * scale
+                c, v = F32(h * math.cos(angle / 2.0)), h * math.sin(angle / 2.0)
+                s = by_half(-v, v)
+            else:
+                c, s = by_half(1.0, math.cos(angle)), by_half(0.0, math.sin(angle))
             if conj:
                 nr, ni = re * c + im * s, re * s - im * c
             else:
                 nr, ni = re * c - im * s, re * s + im * c
         dst[k, rows, 0:LANES] = nr
         dst[k, rows, LANES : 2 * LANES] = ni
+
+
+def inverse_turn(k, re, im):
+    if k == 0:
+        return re, None
+    if k == HALF - 1:
+        lane = lax.broadcasted_iota(jnp.int32, (ROWS, LANES), 1)
+        return jnp.where(lane < SIDE, re, -im), None
+    t = math.tan(math.pi * k / SIDE)
+    if needs_conjugate(k):
+        return re - im * by_half(-t, t), re * by_half(t, -t) - im
+    return re - im * by_half(-t, t), im + re * by_half(-t, t)
 
 
 def split_in_two(x):
@@ -148,9 +165,9 @@
 
 
 def forward_lanes(src, w_ref):
-    x = src[...].reshape(HALF * 2 * ROWS, 2 * LANES)
-    high, low = split_in_two(x)
-    return times_lane_matrix(high, low, w_ref).reshape(HALF, 2 * ROWS, 2 * LANES)
+    tiles, rows, lanes = src.shape
+    high, low = split_in_two(src[...].reshape(tiles * rows, lanes))
+    return times_lane_matrix(high, low, w_ref).reshape(tiles, rows, lanes)
 
 
 def grid_weights(gath, first, count):
@@ -184,9 +201,9 @@
     return jnp.where(some, jnp.log(jnp.where(some, total, 1.0)) / math.log(2.0), FAR)
 
 
-def pair_products(fq, de, first, count, lhs):
+def pair_products(f_ref, q_ref, de, first, count, lhs):
     for k in range(HALF):
-        f, q = fq[k, 0:ROWS, :], fq[k, ROWS : 2 * ROWS, :]
+        f, q = f_ref[k], q_ref[:, k * 2 * LANES : (k + 1) * 2 * LANES]
         fr, fi, qr, qi = f[:, :LANES], f[:, LANES:], q[:, :LANES], q[:, LANES:]
         fd, qd = fr - fi, qr - qi
         parts = []
@@ -213,21 +230,12 @@
 
 
 def scores(g_ref, score_ref, first, count):
-    lane = lax.broadcasted_iota(jnp.int32, (ROWS, LANES), 1)
     for i in range(count):
         rows = pl.ds(i * ROWS, ROWS)
-        spec = []
-        for k in range(HALF):
-            re, im = g_ref[k, rows, 0:LANES], g_ref[k, rows, LANES : 2 * LANES]
-            if k == 0:
-                spec.append((re, None))
-            elif k == HALF - 1:
-                spec.append((jnp.where(lane < SIDE, re, -im), None))
-            else:
-                c, s = lane_turn(k, 1.0)
-                nr = re * c - im * s
-                ni = -(re * s) - im * c if needs_conjugate(k) else re * s + im * c
-                spec.append((nr, ni))
+        spec = [
+            inverse_turn(k, g_ref[k, rows, 0:LANES], g_ref[k, rows, LANES : 2 * LANES])
+            for k in range(HALF)
+        ]
         for j, value in enumerate(inverse_real_dft(spec)):
             score_ref[first + i, j] = value
 
@@ -240,10 +248,10 @@
     return values[0]
 
 
-def log_sums(score_ref, lw_ref, ms_ref, per_step):
-    def some_groups(step, _):
-        for p in range(per_step):
-            i = step * per_step + p
+def log_sums(score_ref, lw_ref, ms_ref, first, end):
+    def one_visit(v, _):
+        for p in range(ROWS):
+            i = v * ROWS + p
             value = [score_ref[i, j] + lw_ref[j : j + 1, :] for j in range(TILES)]
             top = tree(jnp.maximum, value)
             total = tree(jnp.add, [jnp.exp2(v - top) for v in value])
@@ -251,7 +259,7 @@
             ms_ref[i, ROWS : 2 * ROWS, :] = total
         return 0
 
-    lax.fori_loop(0, score_ref.shape[0] // per_step, some_groups, 0)
+    lax.fori_loop(first, end, one_visit, 0)
 
 
 def results(ms_ref):
@@ -289,14 +297,16 @@
     msg,
     gath,
     stage,
-    spec_fq,
+    stage_f,
+    spec_f,
+    spec_q,
     spec_de,
     lhs_a,
     lhs_b,
     g_a,
     g_b,
     score_ref,
-    csq_ref,
+    class_spec,
     early_ref,
     lw_ref,
     ms_ref,
@@ -437,20 +447,26 @@
         blocks[0, :, j * LANES : (j + 1) * LANES] = jnp.concatenate(pair, axis=0).astype(BF16)
     blocks[0, :, half * LANES :] = jnp.concatenate([cls, cls], axis=0).astype(F32).astype(BF16)
 
-    def block_copy(src, dst, to):
-        return pltpu.make_async_remote_copy(
-            src_ref=blocks.at[src],
-            dst_ref=blocks.at[dst],
-            send_sem=block_send_sem.at[2 * src + to - 1],
-            recv_sem=block_recv_sem.at[dst],
-            device_id=(conf_at(to), o),
-            device_id_type=MESH,
-        )
-
-    first_copy, second_copy, passed_copy = (
-        block_copy(0, 1, 1),
-        block_copy(0, 2, 2),
-        block_copy(1, 2, 1),
+    middle = half // 2 * LANES
+    pieces = (pl.ds(0, middle), pl.ds(middle, blocks.shape[2] - middle))
+
+    def block_copies(src, dst, to):
+        return [
+            pltpu.make_async_remote_copy(
+                src_ref=blocks.at[src, :, piece],
+                dst_ref=blocks.at[dst, :, piece],
+                send_sem=block_send_sem.at[2 * src + to - 1, i],
+                recv_sem=block_recv_sem.at[dst, i],
+                device_id=(conf_at(to), o),
+                device_id_type=MESH,
+            )
+            for i, piece in enumerate(pieces)
+        ]
+
+    first_copies, second_copies, passed_copies = (
+        block_copies(0, 1, 1),
+        block_copies(0, 2, 2),
+        block_copies(1, 2, 1),
     )
 
     def send_blocks():
@@ -463,8 +479,13 @@
         def _():
             pl.semaphore_wait(pair_sem, 1)
 
-        first_copy.start()
-        pl.when(jnp.logical_not(last_x))(second_copy.start)
+        for copy in first_copies:
+            copy.start()
+
+        @pl.when(jnp.logical_not(last_x))
+        def _():
+            for copy in second_copies:
+                copy.start()
 
     send_early = b >= n_conf - 2
     pl.when(send_early)(send_blocks)
@@ -487,38 +508,43 @@
             for t in range(LAYER):
                 send_grid(layer * LAYER + t)
 
-    def forward(tiles, other_tiles, scale):
-        forward_rows(tiles, scale, stage, 0)
-        forward_rows(other_tiles, scale, stage, ROWS)
-        return forward_lanes(stage, w_ref)
-
     loads[5].wait()
     loads[6].wait()
     dens = [dens_ref[:, j * LANES : (j + 1) * LANES].astype(F32) for j in range(TILES)]
+    forward_rows(dens, stage, 0)
     excess = [(t * t - 1.0).astype(BF16).astype(F32) for t in dens]
-    de = forward(dens, excess, 1.0)
+    forward_rows(excess, stage, ROWS)
+    de = forward_lanes(stage, w_ref)
     dr, di = de[:, :, :LANES], de[:, :, LANES:]
     spec_de[...] = jnp.concatenate([dr, dr + di, di - dr], axis=2)
-    con = con_ref[...]
-    csq_ref[...] = (con * con).astype(BF16)
+
+    n_cls = con_ref.shape[0]
+    for row in range(0, n_cls, ROWS):
+        squares = []
+        for j in range(TILES):
+            tile = con_ref[row : row + ROWS, j * LANES : (j + 1) * LANES]
+            squares.append((tile * tile).astype(BF16).astype(F32))
+        forward_rows(squares, stage, row, -LOG2E * 2.0**-17, True)
+    of_classes = forward_lanes(stage, w_ref)
+    for k in range(HALF):
+        high, low = split_in_two(of_classes[k])
+        cols = slice(k * 2 * LANES, (k + 1) * 2 * LANES)
+        class_spec[0:n_cls, cols] = high
+        class_spec[n_cls:, cols] = low
 
     def visit(v):
-        n_cls = csq_ref.shape[0]
-        classes = blocks[v, :, half * LANES :].astype(F32)[0:ROWS, 0:n_cls]
-        column = lax.broadcasted_iota(jnp.int32, (ROWS, n_cls), 1).astype(F32)
-        picks = jnp.where(classes == column, 1.0, 0.0).astype(BF16)
-        squares = jnp.dot(picks, csq_ref[...], preferred_element_type=F32)
+        classes = blocks[v, :, half * LANES :].astype(F32)[0:ROWS, 0 : 2 * n_cls]
+        column = lax.broadcasted_iota(jnp.int32, (ROWS, 2 * n_cls), 1) % n_cls
+        picks = jnp.where(classes == column.astype(F32), 1.0, 0.0).astype(BF16)
+        spec_q[...] = jnp.dot(picks, class_spec[...], preferred_element_type=F32)
         pairs = [blocks[v, :, j * LANES : (j + 1) * LANES].astype(F32) for j in range(half)]
         rows = [p[0:ROWS] for p in pairs] + [p[ROWS:] for p in pairs]
-        rows = [r * (LOG2E * 2.0**-16) for r in rows]
-        others = [
-            squares[:, j * LANES : (j + 1) * LANES] * (-LOG2E * 2.0**-17) for j in range(TILES)
-        ]
-        spec_fq[...] = forward(rows, others, 2.0)
+        forward_rows(rows, stage_f, 0, LOG2E * 2.0**-16, True)
+        spec_f[...] = forward_lanes(stage_f, w_ref)
         part = ROWS // 2
-        pair_products(spec_fq, spec_de, 0, part, lhs_a)
+        pair_products(spec_f, spec_q, spec_de, 0, part, lhs_a)
         inverse_lanes(lhs_a, w_ref, g_a)
-        pair_products(spec_fq, spec_de, part, part, lhs_b)
+        pair_products(spec_f, spec_q, spec_de, part, part, lhs_b)
         inverse_lanes(lhs_b, w_ref, g_b)
         scores(g_a, score_ref, v * ROWS, part)
         scores(g_b, score_ref, v * ROWS + part, part)
@@ -547,10 +573,10 @@
             def _():
                 grid_wait(layer, LAYER).wait_recv()
 
-    early = max(n_layers // 2 - 1, 1)
+    early = n_layers // 2
 
     def make_weights():
-        last = (early + n_layers + 1) // 2
+        last = (early + n_layers) // 2
         total = early_ref[...]
         for first, end in ((last, n_layers), (early, last)):
             hear(range(first, end))
@@ -572,24 +598,28 @@
         hear(range(early))
         early_ref[...] = grid_weights(gath, 0, early * LAYER)
 
-    weights_at = jnp.where((x == 1) | ((x == 0) & (z > 0)), 2, 3)
+    weights_at = jnp.where((x == 1) | (z > 0), 2, 3)
+    sums_early = is_hub & (x == 1)
 
     def step(v, _):
-        @pl.when(is_hub & (weights_at == v))
+        pl.when(is_hub & (weights_at == v))(make_weights)
+
+        @pl.when(sums_early & (v == 2))
         def _():
-            make_weights()
+            log_sums(score_ref, lw_ref, ms_ref, 0, 2)
 
         @pl.when(v < 3)
         def _():
-            pltpu.make_async_remote_copy(
-                src_ref=blocks.at[0],
-                dst_ref=blocks.at[v],
-                send_sem=block_send_sem.at[v],
-                recv_sem=block_recv_sem.at[v],
-                device_id=(conf_at(1), o),
-                device_id_type=MESH,
-            ).wait_recv()
-            pl.when((v == 1) & (x == 0))(passed_copy.start)
+            for i, piece in enumerate(pieces):
+                pltpu.make_async_remote_copy(
+                    src_ref=blocks.at[0, :, piece],
+                    dst_ref=blocks.at[v, :, piece],
+                    send_sem=block_send_sem.at[0, i],
+                    recv_sem=block_recv_sem.at[v, i],
+                    device_id=(conf_at(1), o),
+                    device_id_type=MESH,
+                ).wait_recv()
+                pl.when((v == 1) & (x == 0))(passed_copies[i].start)
             visit(v)
 
         return 0
@@ -607,7 +637,7 @@
             device_id_type=MESH,
         ).wait_recv()
 
-    log_sums(score_ref, lw_ref, ms_ref, 4)
+    log_sums(score_ref, lw_ref, ms_ref, jnp.where(sums_early, 2, 0), 3)
     final = results(ms_ref)
     for v in range(3):
         out_ref[v] = final[v * ROWS : (v + 1) * ROWS, :]
@@ -626,9 +656,13 @@
     def _():
         grid_wait(0, LAYER * n_hubs).wait_send()
 
-    first_copy.wait_send()
-    pl.when(jnp.logical_not(last_x))(second_copy.wait_send)
-    pl.when(x == 0)(passed_copy.wait_send)
+    for copies, sent in (
+        (first_copies, x >= 0),
+        (second_copies, jnp.logical_not(last_x)),
+        (passed_copies, x == 0),
+    ):
+        for copy in copies:
+            pl.when(sent)(copy.wait_send)
 
 
 def solution(mesh):
@@ -649,7 +683,6 @@
                 jnp.asarray(w),
             )
         ]
-        spectrum = pltpu.VMEM((HALF, 2 * ROWS, 2 * LANES), F32)
         return pl.pallas_call(
             functools.partial(kernel, n_conf, n_orient),
             out_shape=pltpu.VMEM((3, ROWS, ROWS), F32),
@@ -666,21 +699,23 @@
                 pltpu.VMEM((3, 2 * ROWS, (TILES // 2 + 1) * LANES), BF16),
                 pltpu.VMEM((2, LANES), F32),
                 pltpu.VMEM((n_orient, 2, LANES), F32),
-                spectrum,
-                spectrum,
+                pltpu.VMEM((HALF, 2 * ROWS, 2 * LANES), F32),
+                pltpu.VMEM((HALF, ROWS, 2 * LANES), F32),
+                pltpu.VMEM((HALF, ROWS, 2 * LANES), F32),
+                pltpu.VMEM((ROWS, HALF * 2 * LANES), F32),
                 pltpu.VMEM((HALF, 2 * ROWS, 3 * LANES), F32),
                 pltpu.VMEM((HALF, ROWS * ROWS // 2, 4 * LANES), BF16),
                 pltpu.VMEM((HALF, ROWS * ROWS // 2, 4 * LANES), BF16),
                 pltpu.VMEM((HALF, ROWS * ROWS // 2, 2 * LANES), F32),
                 pltpu.VMEM((HALF, ROWS * ROWS // 2, 2 * LANES), F32),
                 pltpu.VMEM((3 * ROWS, TILES, ROWS, LANES), F32),
-                pltpu.VMEM(contrast.shape, BF16),
+                pltpu.VMEM((2 * contrast.shape[0], HALF * 2 * LANES), BF16),
                 pltpu.VMEM((TILES, LANES), F32),
                 pltpu.VMEM((TILES, LANES), F32),
                 pltpu.VMEM((3 * ROWS, 2 * ROWS, LANES), F32),
                 pltpu.SemaphoreType.DMA((7,)),
-                pltpu.SemaphoreType.DMA((4,)),
-                pltpu.SemaphoreType.DMA((3,)),
+                pltpu.SemaphoreType.DMA((4, 2)),
+                pltpu.SemaphoreType.DMA((3, 2)),
                 pltpu.SemaphoreType.DMA,
                 pltpu.SemaphoreType.DMA((n_orient // LAYER,)),
                 pltpu.SemaphoreType.DMA((n_orient // LAYER,)),

time: 16.6 us -> 16.2 us (0.976)
  Pallas kernels: 15.8 us -> 15.5 us
    pallas_call x1, Pallas kernels: 15.8 us -> 15.5 us  [per_device(): pl.pallas_call(functools.partial(kernel, n_conf, n_orient), out_shape=plt...]
where the time goes in v5:
time: 16.2 us; the launch traced here: 16.1 us
  Pallas kernels  15.5 us (96%)
  local copies, waits for them, and re-layouts  0.6 us (4%)
    pallas_call x1, Pallas kernels, per_device(): pl.pallas_call(functools.partial(kernel, n_conf, n_orient), out_shape=plt...  15.5 us
    unnamed x1, local copies, waits for them, and re-layouts  0.6 us

profile of v5, /device:TPU:1, one launch (start us, length us, event | category | flops | bytes accessed | tf_op | source)
XLA Modules:
  0.0 16.1 jit_solution(7151907060020701047)
XLA Ops:
  0.0 15.5 %shard_map.73 = f32[3,8,8]{2,1,0:T(8,128)S(1)} custom-call(s32[8]{0:T(128)} %cls_hbm.1, bf16[8,4096]{1,0:T(8,128)(2,1)} %part_hbm.1, bf16[8,4096]{1,0:T(8,128)(2,1)} %dens_hbm.1, f32[16,4096]{1,0:T(8,128)} %con_hbm.1, s32[96]{0:T(128)} %shift_hbm.1, f32[96]{0:T(128)} %prior_hbm.1, bf16[512,256]{1,0:T(8,128)(2,1)} %constant.2.clone.w_hbm), custom_call_target="tpu_custom_call" | custom-call | tf_op jit(solution)/shard_map/pallas_call | solution.py:686
  15.5 0.6 %copy.9 = f32[3,8,8]{2,1,0:T(8,128)} copy(f32[3,8,8]{2,1,0:T(8,128)S(1)} %shard_map.73) | data formatting | bytes 1536

commit v6 on v5

--- a/solution.py
+++ b/solution.py
@@ -469,6 +469,8 @@
         block_copies(1, 2, 1),
     )
 
+    far = b == n_conf - 2
+
     def send_blocks():
         @pl.when(core == 1)
         def _():
@@ -482,12 +484,12 @@
         for copy in first_copies:
             copy.start()
 
-        @pl.when(jnp.logical_not(last_x))
+        @pl.when(jnp.logical_not(last_x | far))
         def _():
             for copy in second_copies:
                 copy.start()
 
-    send_early = b >= n_conf - 2
+    send_early = x >= n_conf // 2 - 2
     pl.when(send_early)(send_blocks)
 
     def grid_wait(layer, number):
@@ -590,6 +592,12 @@
 
     visit(0)
     pl.when(jnp.logical_not(send_early))(send_blocks)
+
+    @pl.when(far)
+    def _():
+        for copy in second_copies:
+            copy.start()
+
     for layer in range(1, n_hubs):
         answer(layer)
 
@@ -598,30 +606,33 @@
         hear(range(early))
         early_ref[...] = grid_weights(gath, 0, early * LAYER)
 
-    weights_at = jnp.where((x == 1) | (z > 0), 2, 3)
+    starts_first = (b == 0) & (place < 2)
+    weights_at = jnp.where((x == 1) | (z > 0), 2, 3) - jnp.where(starts_first, 1, 0)
     sums_early = is_hub & (x == 1)
 
+    def hear_block(v):
+        for i, piece in enumerate(pieces):
+            pltpu.make_async_remote_copy(
+                src_ref=blocks.at[0, :, piece],
+                dst_ref=blocks.at[v, :, piece],
+                send_sem=block_send_sem.at[0, i],
+                recv_sem=block_recv_sem.at[v, i],
+                device_id=(conf_at(1), o),
+                device_id_type=MESH,
+            ).wait_recv()
+            if v == 1:
+                pl.when(x == 0)(passed_copies[i].start)
+
     def step(v, _):
+        pl.when(v == 1)(lambda: hear_block(1))
         pl.when(is_hub & (weights_at == v))(make_weights)
 
         @pl.when(sums_early & (v == 2))
         def _():
             log_sums(score_ref, lw_ref, ms_ref, 0, 2)
 
-        @pl.when(v < 3)
-        def _():
-            for i, piece in enumerate(pieces):
-                pltpu.make_async_remote_copy(
-                    src_ref=blocks.at[0, :, piece],
-                    dst_ref=blocks.at[v, :, piece],
-                    send_sem=block_send_sem.at[0, i],
-                    recv_sem=block_recv_sem.at[v, i],
-                    device_id=(conf_at(1), o),
-                    device_id_type=MESH,
-                ).wait_recv()
-                pl.when((v == 1) & (x == 0))(passed_copies[i].start)
-            visit(v)
-
+        pl.when(v == 2)(lambda: hear_block(2))
+        pl.when(v < 3)(lambda: visit(v))
         return 0
 
     lax.fori_loop(1, 4, step, 0)

time: 16.2 us -> 15.6 us (0.963)
  Pallas kernels: 15.5 us -> 14.9 us
    pallas_call x1, Pallas kernels: 15.5 us -> 14.9 us  [per_device(): pl.pallas_call(functools.partial(kernel, n_conf, n_orient), out_shape=plt...]
where the time goes in v6:
time: 15.6 us; the launch traced here: 15.5 us
  Pallas kernels  14.9 us (96%)
  local copies, waits for them, and re-layouts  0.6 us (4%)
    pallas_call x1, Pallas kernels, per_device(): pl.pallas_call(functools.partial(kernel, n_conf, n_orient), out_shape=plt...  14.9 us
    unnamed x1, local copies, waits for them, and re-layouts  0.6 us

profile of v6, /device:TPU:1, one launch (start us, length us, event | category | flops | bytes accessed | tf_op | source)
XLA Modules:
  0.0 15.5 jit_solution(8342139627181980091)
XLA Ops:
  0.0 14.9 %shard_map.73 = f32[3,8,8]{2,1,0:T(8,128)S(1)} custom-call(s32[8]{0:T(128)} %cls_hbm.1, bf16[8,4096]{1,0:T(8,128)(2,1)} %part_hbm.1, bf16[8,4096]{1,0:T(8,128)(2,1)} %dens_hbm.1, f32[16,4096]{1,0:T(8,128)} %con_hbm.1, s32[96]{0:T(128)} %shift_hbm.1, f32[96]{0:T(128)} %prior_hbm.1, bf16[512,256]{1,0:T(8,128)(2,1)} %constant.2.clone.w_hbm), custom_call_target="tpu_custom_call" | custom-call | tf_op jit(solution)/shard_map/pallas_call | solution.py:697
  14.9 0.6 %copy.9 = f32[3,8,8]{2,1,0:T(8,128)} copy(f32[3,8,8]{2,1,0:T(8,128)S(1)} %shard_map.73) | data formatting | bytes 1536

commit v7 on v6

--- a/solution.py
+++ b/solution.py
@@ -368,9 +368,7 @@
         loads.append(pltpu.make_async_copy(src, dst, in_sem.at[i]))
         loads[-1].start()
 
-    @pl.when(core == 1)
-    def _():
-        greet(b, o - 1)
+    greet(b, o + 1 - 2 * core)
 
     @pl.when(is_hub)
     def _():
@@ -391,61 +389,31 @@
     msg[1:2, 0:count] = jnp.exp(prior_ref[...]).reshape(1, count)
     gath[o] = msg[...]
 
-    hubs_below = LAYER * jnp.minimum(z, n_hubs)
-
-    @pl.when(first_core)
-    def _():
-        pl.semaphore_wait(barrier, 1 + hubs_below + jnp.where(is_hub, LAYER - 2, 0))
-        tell_sibling()
-
-    @pl.when(core == 1)
-    def _():
-        pl.semaphore_wait(pair_sem, 1)
-
-    def send_grid(to):
-        pltpu.make_async_remote_copy(
-            src_ref=msg,
-            dst_ref=gath.at[o],
-            send_sem=grid_send_sem,
-            recv_sem=grid_recv_sem.at[z],
-            device_id=(b, to),
-            device_id_type=MESH,
-        ).start()
-
-    def send_below(t, _):
-        send_grid(t)
-        return 0
-
-    def send_beside(t, _):
-        send_grid(z * LAYER + lax.rem(place + t, LAYER))
-        return 0
-
-    lax.fori_loop(0, hubs_below, send_below, 0)
-    lax.fori_loop(1, jnp.where(is_hub, LAYER, 1), send_beside, 0)
-
-    for load in loads[2:5]:
-        load.wait()
-    row = lax.broadcasted_iota(jnp.int32, (ROWS, LANES), 0)
-    cls = jnp.zeros((ROWS, LANES), jnp.int32)
-    for i in range(ROWS):
-        cls = jnp.where(row == i, cls_ref[i], cls)
-
-    picked = [cls == k for k in range(con_ref.shape[0])]
-
-    def envelope(j):
-        out = jnp.zeros((ROWS, LANES), F32)
-        for k, mask in enumerate(picked):
-            out = jnp.where(mask, con_ref[k : k + 1, j * LANES : (j + 1) * LANES], out)
-        return out
-
     half = TILES // 2
-    for j in range(half):
-        pair = [
-            part_ref[:, t * LANES : (t + 1) * LANES].astype(F32) * envelope(t)
-            for t in (j, j + half)
-        ]
-        blocks[0, :, j * LANES : (j + 1) * LANES] = jnp.concatenate(pair, axis=0).astype(BF16)
-    blocks[0, :, half * LANES :] = jnp.concatenate([cls, cls], axis=0).astype(F32).astype(BF16)
+
+    def prepare_block():
+        for load in loads[2:5]:
+            load.wait()
+        row = lax.broadcasted_iota(jnp.int32, (ROWS, LANES), 0)
+        cls = jnp.zeros((ROWS, LANES), jnp.int32)
+        for i in range(ROWS):
+            cls = jnp.where(row == i, cls_ref[i], cls)
+
+        picked = [cls == k for k in range(con_ref.shape[0])]
+
+        def envelope(j):
+            out = jnp.zeros((ROWS, LANES), F32)
+            for k, mask in enumerate(picked):
+                out = jnp.where(mask, con_ref[k : k + 1, j * LANES : (j + 1) * LANES], out)
+            return out
+
+        for j in range(half):
+            pair = [
+                part_ref[:, t * LANES : (t + 1) * LANES].astype(F32) * envelope(t)
+                for t in (j, j + half)
+            ]
+            blocks[0, :, j * LANES : (j + 1) * LANES] = jnp.concatenate(pair, axis=0).astype(BF16)
+        blocks[0, :, half * LANES :] = jnp.concatenate([cls, cls], axis=0).astype(F32).astype(BF16)
 
     middle = half // 2 * LANES
     pieces = (pl.ds(0, middle), pl.ds(middle, blocks.shape[2] - middle))
@@ -469,12 +437,10 @@
         block_copies(1, 2, 1),
     )
 
-    far = b == n_conf - 2
-
     def send_blocks():
         @pl.when(core == 1)
         def _():
-            pl.semaphore_wait(barrier, jnp.where(last_x, 2, 4))
+            pl.semaphore_wait(barrier, jnp.where(last_x, 3, 5))
             tell_sibling()
 
         @pl.when(first_core)
@@ -484,13 +450,53 @@
         for copy in first_copies:
             copy.start()
 
-        @pl.when(jnp.logical_not(last_x | far))
+        @pl.when(jnp.logical_not(last_x))
         def _():
             for copy in second_copies:
                 copy.start()
 
     send_early = x >= n_conf // 2 - 2
-    pl.when(send_early)(send_blocks)
+    at_once = b >= n_conf - 2
+
+    @pl.when(at_once)
+    def _():
+        prepare_block()
+        send_blocks()
+
+    hubs_below = LAYER * jnp.minimum(z, n_hubs)
+
+    @pl.when(first_core)
+    def _():
+        pl.semaphore_wait(barrier, 1 + hubs_below + jnp.where(is_hub, LAYER - 2, 0))
+        tell_sibling()
+
+    @pl.when(core == 1)
+    def _():
+        pl.semaphore_wait(pair_sem, 1)
+
+    def send_grid(to):
+        pltpu.make_async_remote_copy(
+            src_ref=msg,
+            dst_ref=gath.at[o],
+            send_sem=grid_send_sem,
+            recv_sem=grid_recv_sem.at[z],
+            device_id=(b, to),
+            device_id_type=MESH,
+        ).start()
+
+    def send_below(t, _):
+        send_grid(t)
+        return 0
+
+    def send_beside(t, _):
+        send_grid(z * LAYER + lax.rem(place + t, LAYER))
+        return 0
+
+    lax.fori_loop(0, hubs_below, send_below, 0)
+    lax.fori_loop(1, jnp.where(is_hub, LAYER, 1), send_beside, 0)
+
+    pl.when(jnp.logical_not(at_once))(prepare_block)
+    pl.when(send_early & jnp.logical_not(at_once))(send_blocks)
 
     def grid_wait(layer, number):
         slots = gath.at[pl.ds(layer * LAYER, number)]
@@ -592,11 +598,6 @@
 
     visit(0)
     pl.when(jnp.logical_not(send_early))(send_blocks)
-
-    @pl.when(far)
-    def _():
-        for copy in second_copies:
-            copy.start()
 
     for layer in range(1, n_hubs):
         answer(layer)

time: 15.6 us -> 15.5 us (level); the launches traced: 15.5 us -> 15.3 us
  Pallas kernels: 14.9 us -> 14.6 us
    pallas_call x1, Pallas kernels: 14.9 us -> 14.6 us  [per_device(): pl.pallas_call(functools.partial(kernel, n_conf, n_orient), out_shape=plt...]
where the time goes in v7:
time: 15.5 us; the launch traced here: 15.3 us
  Pallas kernels  14.6 us (94%)
  local copies, waits for them, and re-layouts  0.6 us (4%)
    pallas_call x1, Pallas kernels, per_device(): pl.pallas_call(functools.partial(kernel, n_conf, n_orient), out_shape=plt...  14.6 us
    unnamed x1, local copies, waits for them, and re-layouts  0.6 us

profile of v7, /device:TPU:1, one launch (start us, length us, event | category | flops | bytes accessed | tf_op | source)
XLA Modules:
  0.0 15.3 jit_solution(885105440431012712)
XLA Ops:
  0.0 14.6 %shard_map.73 = f32[3,8,8]{2,1,0:T(8,128)S(1)} custom-call(s32[8]{0:T(128)} %cls_hbm.1, bf16[8,4096]{1,0:T(8,128)(2,1)} %part_hbm.1, bf16[8,4096]{1,0:T(8,128)(2,1)} %dens_hbm.1, f32[16,4096]{1,0:T(8,128)} %con_hbm.1, s32[96]{0:T(128)} %shift_hbm.1, f32[96]{0:T(128)} %prior_hbm.1, bf16[512,256]{1,0:T(8,128)(2,1)} %constant.2.clone.w_hbm), custom_call_target="tpu_custom_call" | custom-call | tf_op jit(solution)/shard_map/pallas_call | solution.py:698
  14.7 0.6 %copy.9 = f32[3,8,8]{2,1,0:T(8,128)} copy(f32[3,8,8]{2,1,0:T(8,128)S(1)} %shard_map.73) | data formatting | bytes 1536

commit v8 on v7

--- a/solution.py
+++ b/solution.py
@@ -302,9 +302,7 @@
     spec_q,
     spec_de,
     lhs_a,
-    lhs_b,
     g_a,
-    g_b,
     score_ref,
     class_spec,
     early_ref,
@@ -549,13 +547,9 @@
         rows = [p[0:ROWS] for p in pairs] + [p[ROWS:] for p in pairs]
         forward_rows(rows, stage_f, 0, LOG2E * 2.0**-16, True)
         spec_f[...] = forward_lanes(stage_f, w_ref)
-        part = ROWS // 2
-        pair_products(spec_f, spec_q, spec_de, 0, part, lhs_a)
+        pair_products(spec_f, spec_q, spec_de, 0, ROWS, lhs_a)
         inverse_lanes(lhs_a, w_ref, g_a)
-        pair_products(spec_f, spec_q, spec_de, part, part, lhs_b)
-        inverse_lanes(lhs_b, w_ref, g_b)
-        scores(g_a, score_ref, v * ROWS, part)
-        scores(g_b, score_ref, v * ROWS + part, part)
+        scores(g_a, score_ref, v * ROWS, ROWS)
 
     def lw_copy(layer):
         return pltpu.make_async_remote_copy(
@@ -716,10 +710,8 @@
                 pltpu.VMEM((HALF, ROWS, 2 * LANES), F32),
                 pltpu.VMEM((ROWS, HALF * 2 * LANES), F32),
                 pltpu.VMEM((HALF, 2 * ROWS, 3 * LANES), F32),
-                pltpu.VMEM((HALF, ROWS * ROWS // 2, 4 * LANES), BF16),
-                pltpu.VMEM((HALF, ROWS * ROWS // 2, 4 * LANES), BF16),
-                pltpu.VMEM((HALF, ROWS * ROWS // 2, 2 * LANES), F32),
-                pltpu.VMEM((HALF, ROWS * ROWS // 2, 2 * LANES), F32),
+                pltpu.VMEM((HALF, ROWS * ROWS, 4 * LANES), BF16),
+                pltpu.VMEM((HALF, ROWS * ROWS, 2 * LANES), F32),
                 pltpu.VMEM((3 * ROWS, TILES, ROWS, LANES), F32),
                 pltpu.VMEM((2 * contrast.shape[0], HALF * 2 * LANES), BF16),
                 pltpu.VMEM((TILES, LANES), F32),

time: 15.5 us -> 15.4 us (level)
  no operation moved by 1% of the time
where the time goes in v8:
time: 15.4 us; the launch traced here: 15.1 us
  Pallas kernels  14.5 us (94%)
  local copies, waits for them, and re-layouts  0.6 us (4%)
    pallas_call x1, Pallas kernels, per_device(): pl.pallas_call(functools.partial(kernel, n_conf, n_orient), out_shape=plt...  14.5 us
    unnamed x1, local copies, waits for them, and re-layouts  0.6 us

profile of v8, /device:TPU:1, one launch (start us, length us, event | category | flops | bytes accessed | tf_op | source)
XLA Modules:
  0.0 15.1 jit_solution(11963753079815860778)
XLA Ops:
  0.0 14.5 %shard_map.73 = f32[3,8,8]{2,1,0:T(8,128)S(1)} custom-call(s32[8]{0:T(128)} %cls_hbm.1, bf16[8,4096]{1,0:T(8,128)(2,1)} %part_hbm.1, bf16[8,4096]{1,0:T(8,128)(2,1)} %dens_hbm.1, f32[16,4096]{1,0:T(8,128)} %con_hbm.1, s32[96]{0:T(128)} %shift_hbm.1, f32[96]{0:T(128)} %prior_hbm.1, bf16[512,256]{1,0:T(8,128)(2,1)} %constant.2.clone.w_hbm), custom_call_target="tpu_custom_call" | custom-call | tf_op jit(solution)/shard_map/pallas_call | solution.py:692
  14.5 0.6 %copy.9 = f32[3,8,8]{2,1,0:T(8,128)} copy(f32[3,8,8]{2,1,0:T(8,128)S(1)} %shard_map.73) | data formatting | bytes 1536

commit v9 on v8

--- a/solution.py
+++ b/solution.py
@@ -578,7 +578,7 @@
     early = n_layers // 2
 
     def make_weights():
-        last = (early + n_layers) // 2
+        last = early + 1
         total = early_ref[...]
         for first, end in ((last, n_layers), (early, last)):
             hear(range(first, end))

time: 15.4 us -> 15.4 us (level)
  no operation moved by 1% of the time
where the time goes in v9:
time: 15.4 us; the launch traced here: 15.1 us
  Pallas kernels  14.5 us (94%)
  local copies, waits for them, and re-layouts  0.6 us (4%)
    pallas_call x1, Pallas kernels, per_device(): pl.pallas_call(functools.partial(kernel, n_conf, n_orient), out_shape=plt...  14.5 us
    unnamed x1, local copies, waits for them, and re-layouts  0.6 us

profile of v9, /device:TPU:1, one launch (start us, length us, event | category | flops | bytes accessed | tf_op | source)
XLA Modules:
  0.0 15.1 jit_solution(16107864549433272177)
XLA Ops:
  0.0 14.5 %shard_map.73 = f32[3,8,8]{2,1,0:T(8,128)S(1)} custom-call(s32[8]{0:T(128)} %cls_hbm.1, bf16[8,4096]{1,0:T(8,128)(2,1)} %part_hbm.1, bf16[8,4096]{1,0:T(8,128)(2,1)} %dens_hbm.1, f32[16,4096]{1,0:T(8,128)} %con_hbm.1, s32[96]{0:T(128)} %shift_hbm.1, f32[96]{0:T(128)} %prior_hbm.1, bf16[512,256]{1,0:T(8,128)(2,1)} %constant.2.clone.w_hbm), custom_call_target="tpu_custom_call" | custom-call | tf_op jit(solution)/shard_map/pallas_call | solution.py:692
  14.5 0.6 %copy.9 = f32[3,8,8]{2,1,0:T(8,128)} copy(f32[3,8,8]{2,1,0:T(8,128)S(1)} %shard_map.73) | data formatting | bytes 1536
